TPU v7x, 1024 devices: a whole 4x4x32 slice. The times are simulated.
1024 devices in a mesh: dp: 16 (over x, y), expert: 64 (over z, core).
Axes of the slice: x: 4, y: 4, z: 32, core: 2. Of those that a mesh axis runs over, the one named last changes fastest.
Arguments:
- tokens: bfloat16 [1024, 196, 768], P(('dp', 'expert')), may hold values from -24 to 24, as said below
- router: bfloat16 [768, 64], replicated, may hold values from -1 to 1, as said below
- w_in: bfloat16 [64, 768, 3072], P('expert', None, 'dp'), may hold values from -0.21875 to 0.21875
- w_out: bfloat16 [64, 3072, 768], P('expert', 'dp'), may hold values from -0.109375 to 0.109375
- out_grad: bfloat16 [1024, 196, 768], P(('dp', 'expert')), may hold values from -6 to 6
Outputs:
- token_grad: bfloat16 [1024, 196, 768], P(('dp', 'expert'))
- router_grad: float32 [768, 64], replicated
- w_in_grad: float32 [64, 768, 3072], P('expert', None, 'dp')
- w_out_grad: float32 [64, 3072, 768], P('expert', 'dp')
Inputs may be any that keep to these rules, and one draw needn't show every extreme that they name: Entries of the tokens stay within the bounds. `router`: entries of the slot parameters stay within the bounds.
All inputs are finite; a program needn't handle non-finite values.
Results may differ from a plain program's by a relative error of at most 0.022.
Values may be sent and summed in bfloat16 or wider, within the bound.
No kernel may reach another device: no remote copies, remote signals or barrier semaphores. Data moves between devices by JAX's collectives and lax.ppermute only.
A program may use at most 32 MiB of HBM per device.

v0:
```python
import jax
import jax.numpy as jnp
from jax import lax
from jax.sharding import PartitionSpec as P


def gelu_exact(value):
    return 0.5 * value * (1.0 + jax.scipy.special.erf(value * 0.7071067811865476))


def gelu_slope(value):
    return (
        0.5 * (1.0 + jax.scipy.special.erf(value * 0.7071067811865476))
        + value * jnp.exp(-0.5 * value * value) * 0.3989422804014327
    )


def per_device(tokens, router, w_in, w_out, out_grad):
    width = tokens.shape[2]
    logits = jnp.einsum("bmd,de->bme", tokens, router, preferred_element_type=jnp.float32)
    dispatch = jax.nn.softmax(logits, axis=1)
    combine = jax.nn.softmax(logits, axis=2)
    dispatch_b = dispatch.astype(jnp.bfloat16)
    combine_b = combine.astype(jnp.bfloat16)
    slots = jnp.einsum(
        "bme,bmd->bed", dispatch_b, tokens, preferred_element_type=jnp.float32
    ).astype(jnp.bfloat16)
    slot_grad = jnp.einsum(
        "bme,bmd->bed", combine_b, out_grad, preferred_element_type=jnp.float32
    ).astype(jnp.bfloat16)
    sent_slots, sent_grads = (
        lax.all_to_all(slots, "expert", split_axis=1, concat_axis=0, tiled=True),
        lax.all_to_all(slot_grad, "expert", split_axis=1, concat_axis=0, tiled=True),
    )
    rows_in, rows_grad = (
        lax.all_gather(sent_slots.reshape(-1, width), "dp", axis=0, tiled=True),
        lax.all_gather(sent_grads.reshape(-1, width), "dp", axis=0, tiled=True),
    )
    first = w_in[0]
    second = w_out[0]
    hidden = jnp.dot(rows_in, first, preferred_element_type=jnp.float32)
    act = gelu_exact(hidden).astype(jnp.bfloat16)
    partial_out = jnp.dot(act, second, preferred_element_type=jnp.float32)
    act_grad = jnp.einsum("rd,fd->rf", rows_grad, second, preferred_element_type=jnp.float32)
    pre_grad = (act_grad * gelu_slope(hidden)).astype(jnp.bfloat16)
    out_weight_grad = jnp.einsum("rf,rd->fd", act, rows_grad, preferred_element_type=jnp.float32)
    in_weight_grad = jnp.einsum("rd,rf->df", rows_in, pre_grad, preferred_element_type=jnp.float32)
    partial_in = jnp.einsum("rf,df->rd", pre_grad, first, preferred_element_type=jnp.float32)
    out_sum, in_sum = (
        lax.psum_scatter(
            partial_out.astype(jnp.bfloat16), "dp", scatter_dimension=0, tiled=True
        ).astype(jnp.float32),
        lax.psum_scatter(
            partial_in.astype(jnp.bfloat16), "dp", scatter_dimension=0, tiled=True
        ).astype(jnp.float32),
    )
    out_rows = out_sum.astype(jnp.bfloat16)
    in_rows = in_sum.astype(jnp.bfloat16)
    expert_out, slot_in_grad = (
        lax.all_to_all(
            out_rows.reshape(-1, 1, width), "expert", split_axis=0, concat_axis=1, tiled=True
        ),
        lax.all_to_all(
            in_rows.reshape(-1, 1, width), "expert", split_axis=0, concat_axis=1, tiled=True
        ),
    )
    combine_dot = jnp.einsum(
        "bmd,bed->bme", out_grad, expert_out, preferred_element_type=jnp.float32
    )
    combine_part = combine * (combine_dot - jnp.sum(combine * combine_dot, axis=2, keepdims=True))
    dispatch_dot = jnp.einsum(
        "bmd,bed->bme", tokens, slot_in_grad, preferred_element_type=jnp.float32
    )
    dispatch_part = dispatch * (
        dispatch_dot - jnp.sum(dispatch * dispatch_dot, axis=1, keepdims=True)
    )
    logit_grad = (combine_part + dispatch_part).astype(jnp.bfloat16)
    token_grad = jnp.einsum("bme,de->bmd", logit_grad, router, preferred_element_type=jnp.float32)
    token_grad = token_grad + jnp.einsum(
        "bme,bed->bmd", dispatch_b, slot_in_grad, preferred_element_type=jnp.float32
    )
    router_local = jnp.einsum("bmd,bme->de", tokens, logit_grad, preferred_element_type=jnp.float32)
    router_grad = lax.psum(router_local, ("dp", "expert"))
    return (
        token_grad.astype(jnp.bfloat16),
        router_grad,
        in_weight_grad[None],
        out_weight_grad[None],
    )


def solution(mesh):
    return jax.shard_map(
        per_device,
        mesh=mesh,
        in_specs=(
            P(("dp", "expert"), None, None),
            P(),
            P("expert", None, "dp"),
            P("expert", "dp", None),
            P(("dp", "expert"), None, None),
        ),
        out_specs=(
            P(("dp", "expert"), None, None),
            P(),
            P("expert", None, "dp"),
            P("expert", "dp", None),
        ),
        check_vma=False,
    )
```

profile of v0, /device:TPU:1, one launch (start us, length us, event | category | flops | bytes accessed | tf_op | source)
XLA Modules:
  0.0 1349.7 jit_solution(15819400487669650909)
XLA Ops:
  7.2 0.0 copy-start
  7.2 0.0 copy-start.4
  7.2 0.0 all-gather.5.cloned.1.call-start
  7.2 0.9 copy-done
  8.1 1.2 fusion.55
  9.4 0.2 fusion.46
  9.6 0.2 fusion.22
  9.8 0.2 copy.38
  10.0 0.5 broadcast.42
  10.5 1.2 reduce.13
  11.7 0.0 copy-start.2
  11.8 58.2 %all_to_all.16 = bf16[64,2,384]{2,1,0:T(2,128)(2,1)S(1)} all-to-all(bf16[64,2,384]{2,1,0:T(2,128)(2,1)S(1)} %reshape.133), channel_id=1, replica_groups=mesh['dp'=16,'expert'=64] {'expert'}, dimensions={0} | all-to-all | bytes 196608 | tf_op jit(solution)/shard_map/all_to_all | solution.py:32
  70.0 0.1 reshape.134
  70.1 0.7 copy.14
  70.7 0.0 all-gather.5.cloned.1.call-update
  70.8 0.0 all-gather.7.cloned.1.call-start
  70.8 0.0 copy-done.4
  70.8 0.2 fusion.23
  71.0 0.2 copy.37
  71.2 1.2 reduce.12
  72.4 33.4 %all_to_all.17 = bf16[64,2,384]{2,1,0:T(2,128)(2,1)S(1)} all-to-all(bf16[64,2,384]{2,1,0:T(2,128)(2,1)S(1)} %reshape.131), channel_id=1, replica_groups=mesh['dp'=16,'expert'=64] {'expert'}, dimensions={0} | all-to-all | bytes 196608 | tf_op jit(solution)/shard_map/all_to_all | solution.py:33
  105.8 0.1 reshape.132
  105.9 0.7 copy.17
  106.5 0.0 copy-start.5
  106.5 0.0 all-gather.7.cloned.1.call-update
  106.5 0.0 reduce-scatter.5.cloned.1.call-start
  106.6 25.4 %all-gather.5.cloned.1.call-done = bf16[1,1024,768]{2,1,0:T(8,128)(2,1)} async-done(((bf16[1,64,768]{2,1,0:T(8,128)(2,1)}), bf16[1,1024,768]{2,1,0:T(8,128)(2,1)}) %all-gather.5.cloned.1.call-update) | async-done | bytes 1572880 | tf_op jit(solution)/shard_map/all_gather | solution.py:36
  131.9 0.0 copy-done.2
  132.0 2.1 multiply_convert_fusion
  134.0 82.1 %all-gather.7.cloned.1.call-done = bf16[1,1024,768]{2,1,0:T(8,128)(2,1)} async-done(((bf16[1,64,768]{2,1,0:T(8,128)(2,1)}), bf16[1,1024,768]{2,1,0:T(8,128)(2,1)}) %all-gather.7.cloned.1.call-update) | async-done | bytes 1572880 | tf_op jit(solution)/shard_map/all_gather | solution.py:37
  216.2 0.0 copy-done.5
  216.2 2.1 fusion.17
  218.3 1.8 convolution_convert_fusion
  220.1 0.0 reduce-scatter.5.cloned.1.call-update
  220.1 0.0 reduce-scatter.3.cloned.1.call-start
  220.2 1.8 convolution_convert_fusion.1
  222.0 0.0 reduce-scatter.3.cloned.1.call-update
  222.0 107.9 %reduce-scatter.5.cloned.1.call-done = bf16[64,768]{1,0:T(8,128)(2,1)} async-done(((bf16[1024,768]{1,0:T(8,128)(2,1)}), bf16[64,768]{1,0:T(8,128)(2,1)}) %reduce-scatter.5.cloned.1.call-update) | async-done | bytes 98320 | tf_op jit(solution)/shard_map/reduce_scatter | solution.py:53
  329.9 1.6 reduce.14
  331.5 0.7 reshape.135
  332.1 25.4 %all-to-all-start.3 = ((bf16[64,2,384]{2,1,0:T(2,128)(2,1)}), bf16[64,2,384]{2,1,0:T(2,128)(2,1)S(1)}, u32[]{:S(2)}, u32[]{:S(2)}) async-start(bf16[64,2,384]{2,1,0:T(2,128)(2,1)} %reshape.135), calls=%async_computation.5 | async-start | bytes 196608 | tf_op jit(solution)/shard_map/all_to_all | solution.py:63
  357.6 86.5 %reduce-scatter.3.cloned.1.call-done = bf16[64,768]{1,0:T(8,128)(2,1)} async-done(((bf16[1024,768]{1,0:T(8,128)(2,1)}), bf16[64,768]{1,0:T(8,128)(2,1)}) %reduce-scatter.3.cloned.1.call-update) | async-done | bytes 98320 | tf_op jit(solution)/shard_map/reduce_scatter | solution.py:50
  444.1 0.0 copy-start.1
  444.1 1.7 reduce.15
  445.8 0.7 reshape.137
  446.4 0.0 all-to-all-done.3
  446.4 25.4 %all-to-all-start.1 = ((bf16[64,2,384]{2,1,0:T(2,128)(2,1)}), bf16[64,2,384]{2,1,0:T(2,128)(2,1)S(1)}, u32[]{:S(2)}, u32[]{:S(2)}) async-start(bf16[64,2,384]{2,1,0:T(2,128)(2,1)} %reshape.137), calls=%async_computation.2 | async-start | bytes 196608 | tf_op jit(solution)/shard_map/all_to_all | solution.py:60
  471.9 0.0 all-reduce.2.cloned.1.call-start
  471.9 2.7 fusion.14
  474.6 0.0 copy-done.1
  474.6 1.3 fusion.11
  475.9 0.1 reshape.136
  476.0 0.2 convolution_bitcast_fusion.1
  476.2 23.7 %all-to-all-done.1 = bf16[64,2,384]{2,1,0:T(2,128)(2,1)S(1)} async-done(((bf16[64,2,384]{2,1,0:T(2,128)(2,1)}), bf16[64,2,384]{2,1,0:T(2,128)(2,1)S(1)}, u32[]{:S(2)}, u32[]{:S(2)}) %all-to-all-start.1) | async-done | bytes 98336 | tf_op jit(solution)/shard_map/all_to_all | solution.py:60
  499.9 0.1 reshape.138
  500.0 0.3 multiply_reduce_fusion.1
  500.2 0.1 add_convert_fusion
  500.3 0.9 convolution_bitcast_fusion
  501.2 0.0 copy-done.3
  501.2 0.3 fusion.56
  501.5 0.0 all-reduce.2.cloned.1.call-update
  501.5 1.1 fusion.21
  502.6 839.0 %all-reduce.2.cloned.1.call-done = f32[768,64]{0,1:T(8,128)} async-done(((f32[768,64]{0,1:T(8,128)}), f32[768,64]{0,1:T(8,128)}) %all-reduce.2.cloned.1.call-update) | async-done | bytes 196624 | tf_op jit(solution)/shard_map/psum | solution.py:83
  1341.5 1.6 copy.42
  (3 shorter events, 0.1 us)
Async XLA Ops:
  7.2 1.0 copy-start
  7.2 63.6 %copy-start.4 = (bf16[1,196,768]{2,1,0:T(8,128)(2,1)S(1)}, bf16[1,196,768]{2,1,0:T(8,128)(2,1)}, u32[]{:S(2)}) copy-start(bf16[1,196,768]{2,1,0:T(8,128)(2,1)} %param.9) | copy-start | bytes 903172
  7.2 124.8 %all-gather.5.cloned.1.call-start = ((), (), s32[]{:S(2)}) async-start(), calls=%async_computation.9 | async-start | bytes 1671168 | tf_op jit(solution)/shard_map/all_gather | solution.py:36
  11.7 120.2 %copy-start.2 = (bf16[1,768,192]{1,2,0:T(8,128)(2,1)S(1)}, bf16[1,768,192]{1,2,0:T(8,128)(2,1)}, u32[]{:S(2)}) copy-start(bf16[1,768,192]{1,2,0:T(8,128)(2,1)} %param.7) | copy-start | bytes 884740
  70.8 145.4 %all-gather.7.cloned.1.call-start = ((), (), s32[]{:S(2)}) async-start(), calls=%async_computation.10 | async-start | bytes 1671168 | tf_op jit(solution)/shard_map/all_gather | solution.py:37
  106.5 109.7 %copy-start.5 = (bf16[1,192,768]{2,1,0:T(8,128)(2,1)S(1)}, bf16[1,192,768]{2,1,0:T(8,128)(2,1)}, u32[]{:S(2)}) copy-start(bf16[1,192,768]{2,1,0:T(8,128)(2,1)} %param.8) | copy-start | bytes 884740
  106.5 223.3 %reduce-scatter.5.cloned.1.call-start = ((), (), s32[]{:S(2)}) async-start(), calls=%async_computation.7 | async-start | bytes 1671168 | tf_op jit(solution)/shard_map/reduce_scatter | solution.py:53
  220.1 224.0 %reduce-scatter.3.cloned.1.call-start = ((), (), s32[]{:S(2)}) async-start(), calls=%async_computation.6 | async-start | bytes 1671168 | tf_op jit(solution)/shard_map/reduce_scatter | solution.py:50
  332.1 114.3 %all-to-all-start.3 = ((bf16[64,2,384]{2,1,0:T(2,128)(2,1)}), bf16[64,2,384]{2,1,0:T(2,128)(2,1)S(1)}, u32[]{:S(2)}, u32[]{:S(2)}) async-start(bf16[64,2,384]{2,1,0:T(2,128)(2,1)} %reshape.135), calls=%async_computation.5 | async-start | bytes 196608 | tf_op jit(solution)/shard_map/all_to_all | solution.py:63
  444.1 30.5 %copy-start.1 = (bf16[1,1024,768]{2,1,0:T(8,128)(2,1)S(1)}, bf16[1,1024,768]{2,1,0:T(8,128)(2,1)}, u32[]{:S(2)}) copy-start(bf16[1,1024,768]{2,1,0:T(8,128)(2,1)} %all-gather.5.cloned.1.call-done) | copy-start | bytes 4718596
  446.4 53.4 %all-to-all-start.1 = ((bf16[64,2,384]{2,1,0:T(2,128)(2,1)}), bf16[64,2,384]{2,1,0:T(2,128)(2,1)S(1)}, u32[]{:S(2)}, u32[]{:S(2)}) async-start(bf16[64,2,384]{2,1,0:T(2,128)(2,1)} %reshape.137), calls=%async_computation.2 | async-start | bytes 196608 | tf_op jit(solution)/shard_map/all_to_all | solution.py:60
  471.9 869.7 %all-reduce.2.cloned.1.call-start = ((), (), s32[]{:S(2)}) async-start(), calls=%async_computation.8 | async-start | bytes 393216 | tf_op jit(solution)/shard_map/psum | solution.py:83
  475.9 25.3 %copy-start.3 = (bf16[768,64]{0,1:T(8,128)(2,1)S(1)}, bf16[768,64]{0,1:T(8,128)(2,1)}, u32[]{:S(2)}) copy-start(bf16[768,64]{0,1:T(8,128)(2,1)} %param.6) | copy-start | bytes 294916
Sparse Core Ops, SparseCore 0:
  70.9 61.0 all-gather.4
  136.7 79.3 all-gather.6
  221.4 108.3 reduce-scatter.4
  335.0 109.0 reduce-scatter.2
  501.6 839.8 all-reduce.1
where the time goes:
time: 1350 us
  waiting for transfers between devices  1160 us (86%)
  blocking collectives  91.6 us (7%)
  starting transfers between devices  51 us (4%)
  matrix products  16.1 us (1%)
  between operations  13.9 us (1%)
    psum x1, waiting for transfers between devices, per_device(): router_grad = lax.psum(router_local, ('dp', 'expert'))  839 us
    reduce_scatter x1, waiting for transfers between devices, per_device(): lax.psum_scatter(partial_in.astype(jnp.bfloat16), 'dp', scatter_dimension...  108 us
    reduce_scatter x1, waiting for transfers between devices, per_device(): lax.psum_scatter(partial_out.astype(jnp.bfloat16), 'dp', scatter_dimensio...  86.5 us
    all_gather x1, waiting for transfers between devices, per_device(): lax.all_gather(sent_grads.reshape(-1, width), 'dp', axis=0, tiled=True)  82.1 us
    all_to_all x1, blocking collectives, per_device(): lax.all_to_all(slots, 'expert', split_axis=1, concat_axis=0, tiled=True)  58.2 us
    all_to_all x1, blocking collectives, per_device(): lax.all_to_all(slot_grad, 'expert', split_axis=1, concat_axis=0, tiled=True)  33.4 us
  transfers between devices with their start and end apart: 7, of which 6 were waited for; matrix products, arithmetic and copies ran while one was open for 1% of the time, Pallas kernels for 0%

commit v1 on v0

v1 whole, which is shorter than its diff:
```python
import jax
import jax.numpy as jnp
import numpy as np
from jax import lax
from jax.sharding import Mesh
from jax.sharding import PartitionSpec as P

BF = jnp.bfloat16
F32 = jnp.float32
ALL = ("x", "y", "z", "c")


def gelu_exact(value):
    return 0.5 * value * (1.0 + jax.scipy.special.erf(value * 0.7071067811865476))


def gelu_slope(value):
    return (
        0.5 * (1.0 + jax.scipy.special.erf(value * 0.7071067811865476))
        + value * jnp.exp(-0.5 * value * value) * 0.3989422804014327
    )


def exchange(parts, axes):
    return lax.all_to_all(parts, axes, split_axis=0, concat_axis=0, tiled=True)


def spread(mine, axes, count):
    return exchange(jnp.broadcast_to(mine[None], (count, *mine.shape)), axes)


def dot(a, b, dims):
    return lax.dot_general(a, b, (dims, ((), ())), preferred_element_type=F32)


def sum_of_all(local, nx, ny, nz, nc):
    experts, width = local.shape
    plane = nx * ny * nc
    pieces = local.astype(BF).reshape(plane, experts // plane, width)
    mine = exchange(pieces, ("x", "y", "c")).astype(F32).sum(axis=0).astype(BF)
    total = spread(mine, "z", nz).astype(F32).sum(axis=0).astype(BF)
    return spread(total, ("x", "y", "c"), plane).reshape(experts, width).astype(F32)


def per_device(nx, ny, nz, nc, tokens, router, w_in, w_out, out_grad):
    tok, og = tokens[0], out_grad[0]
    width = tok.shape[1]
    experts = nz * nc
    block = w_in.shape[2]

    weights = jnp.concatenate([w_in[0].T, w_out[0]], axis=0)
    gathered = lax.all_gather(weights, "x", axis=0, tiled=False)
    first = gathered[:, :block].reshape(nx * block, width)
    second = gathered[:, block:].reshape(nx * block, width)

    logits = jnp.dot(tok, router, preferred_element_type=F32)
    dispatch = jax.nn.softmax(logits, axis=0)
    combine = jax.nn.softmax(logits, axis=1)
    dispatch_b = dispatch.astype(BF)
    combine_b = combine.astype(BF)
    slots = dot(dispatch_b, tok, ((0,), (0,))).astype(BF)
    slot_grad = dot(combine_b, og, ((0,), (0,))).astype(BF)
    sent = jnp.stack([slots, slot_grad], axis=1)
    mine = exchange(sent, ("z", "c"))
    pair = jnp.stack([mine[:, 0], mine[:, 1]], axis=0)
    rows = spread(pair, "y", ny)
    rows_in = rows[:, 0].reshape(ny * experts, width)
    rows_grad = rows[:, 1].reshape(ny * experts, width)

    hidden = dot(rows_in, first, ((1,), (1,)))
    act = gelu_exact(hidden).astype(BF)
    act_grad = dot(rows_grad, second, ((1,), (1,)))
    pre_grad = (act_grad * gelu_slope(hidden)).astype(BF)
    partial_out = dot(act, second, ((1,), (0,))).astype(BF)
    partial_in = dot(pre_grad, first, ((1,), (0,))).astype(BF)
    partial = jnp.stack(
        [partial_out.reshape(ny, experts, width), partial_in.reshape(ny, experts, width)], axis=1
    )
    summed = exchange(partial, "y").astype(F32).sum(axis=0).astype(BF)
    back = exchange(jnp.stack([summed[0], summed[1]], axis=1), ("z", "c"))
    expert_out, slot_in_grad = back[:, 0], back[:, 1]

    out_part = dot(act, rows_grad, ((0,), (0,))).reshape(nx, block, width)
    in_part = dot(pre_grad, rows_in, ((0,), (0,))).reshape(nx, block, width)
    parts = jnp.concatenate([in_part, out_part], axis=1)
    grads = lax.psum_scatter(parts.astype(BF), "x", scatter_dimension=0, tiled=False).astype(F32)

    combine_dot = dot(og, expert_out, ((1,), (1,)))
    combine_part = combine * (combine_dot - jnp.sum(combine * combine_dot, axis=1, keepdims=True))
    dispatch_dot = dot(tok, slot_in_grad, ((1,), (1,)))
    dispatch_part = dispatch * (
        dispatch_dot - jnp.sum(dispatch * dispatch_dot, axis=0, keepdims=True)
    )
    logit_grad = (combine_part + dispatch_part).astype(BF)
    router_local = dot(logit_grad, tok, ((0,), (0,)))
    router_grad = sum_of_all(router_local, nx, ny, nz, nc).T
    token_grad = dot(logit_grad, router, ((1,), (1,))) + dot(
        dispatch_b, slot_in_grad, ((1,), (0,))
    )
    return token_grad.astype(BF)[None], router_grad, grads[:block].T[None], grads[block:][None]


def solution(mesh):
    dp, expert = mesh.shape["dp"], mesh.shape["expert"]
    nx, ny, nz, nc = 4, dp // 4, expert // 2, 2
    fine = Mesh(np.asarray(mesh.devices).reshape(nx, ny, nz, nc), ALL)

    def run(*args):
        return per_device(nx, ny, nz, nc, *args)

    return jax.shard_map(
        run,
        mesh=fine,
        in_specs=(
            P(ALL, None, None),
            P(),
            P(("z", "c"), None, ("x", "y")),
            P(("z", "c"), ("x", "y"), None),
            P(ALL, None, None),
        ),
        out_specs=(
            P(ALL, None, None),
            P(),
            P(("z", "c"), None, ("x", "y")),
            P(("z", "c"), ("x", "y"), None),
        ),
        check_vma=False,
    )
```

time: 1350 us -> 229 us (0.17)
  waiting for transfers between devices: 1160 us -> 34.1 us
  blocking collectives: 91.6 us -> 152 us
  starting transfers between devices: 51 us -> 9.27 us
    psum x1 -> x0, waiting for transfers between devices: 839 us -> none  [per_device(): router_grad = lax.psum(router_local, ('dp', 'expert'))]
    reduce_scatter x2 -> x1, waiting for transfers between devices: 194 us -> 0.01 us  [per_device(): lax.psum_scatter(parts.astype(BF), 'x', scatter_dimension=0, tiled=False)]
    all_gather x2 -> x1, waiting for transfers between devices: 107 us -> 0.02 us  [per_device(): gathered = lax.all_gather(weights, 'x', axis=0, tiled=False)]
    all_to_all x2 -> x5, blocking collectives: 91.6 us -> 152 us  [exchange(): return lax.all_to_all(parts, axes, split_axis=0, concat_axis=0, tiled=True)]
    all_to_all x2, starting transfers between devices: 50.8 us -> 9.19 us  [exchange(): return lax.all_to_all(parts, axes, split_axis=0, concat_axis=0, tiled=True)]
  transfers between devices with their start and end apart: 7 -> 4, of which waited for: 6 -> 2; matrix products, arithmetic and copies ran while one was open for 1% -> 3% of each run, Pallas kernels for 0% -> 0%
where the time goes in v1:
time: 229 us
  blocking collectives  152 us (66%)
  waiting for transfers between devices  34.1 us (15%)
  between operations  14.3 us (6%)
  starting transfers between devices  9.27 us (4%)
  local copies, waits for them, and re-layouts  7.11 us (3%)
  matrix products  6.1 us (3%)
  other arithmetic  5.52 us (2%)
    all_to_all x5, blocking collectives, exchange(): return lax.all_to_all(parts, axes, split_axis=0, concat_axis=0, tiled=True)  152 us
    all_to_all x2, waiting for transfers between devices, exchange(): return lax.all_to_all(parts, axes, split_axis=0, concat_axis=0, tiled=True)  34.1 us
    all_to_all x2, starting transfers between devices, exchange(): return lax.all_to_all(parts, axes, split_axis=0, concat_axis=0, tiled=True)  9.19 us
    dot_general x13, matrix products, dot(): return lax.dot_general(a, b, (dims, ((), ())), preferred_element_type=F32)  5.76 us
  transfers between devices with their start and end apart: 4, of which 2 were waited for; matrix products, arithmetic and copies ran while one was open for 3% of the time, Pallas kernels for 0%

profile of v1, /device:TPU:1, one launch (start us, length us, event | category | flops | bytes accessed | tf_op | source)
XLA Modules:
  0.0 228.8 jit_solution(9473380736332354794)
XLA Ops:
  7.2 0.0 copy-start
  7.2 0.0 copy-start.2
  7.2 0.0 copy-start.3
  7.2 0.0 all-gather.3.cloned.1.call-start
  7.2 2.0 pad_maximum_fusion.2
  9.2 0.0 all-gather.3.cloned.1.call-update
  9.2 0.0 reduce-scatter.2.cloned.1.call-start
  9.3 0.0 copy-done
  9.3 0.0 copy-done.2
  9.3 0.3 fusion.46
  9.6 0.2 fusion.35
  9.8 0.0 copy-done.3
  9.9 0.2 fusion.3
  10.0 0.2 fusion.2
  10.3 0.2 copy.40
  10.5 66.8 %all_to_all.35 = bf16[64,2,768]{2,1,0:T(2,128)(2,1)S(1)} all-to-all(bf16[64,2,768]{2,1,0:T(2,128)(2,1)S(1)} %copy.40), channel_id=1, replica_groups=mesh['x'=4,'y'=4,'z'=32,'c'=2] {'z','c'}, dimensions={0} | all-to-all | bytes 393216 | tf_op jit(solution)/shard_map/all_to_all | solution.py:25
  77.4 0.3 fusion.50
  77.7 0.1 broadcast_in_dim.10
  77.8 14.5 %all_to_all.36 = bf16[4,2,64,768]{3,2,1,0:T(8,128)(2,1)S(1)} all-to-all(bf16[4,2,64,768]{3,2,1,0:T(8,128)(2,1)S(1)} %broadcast_in_dim.10), channel_id=1, replica_groups=mesh['x'=4,'y'=4,'z'=32,'c'=2] {'y'}, dimensions={0} | all-to-all | bytes 1572864 | tf_op jit(solution)/shard_map/all_to_all | solution.py:25
  92.3 0.1 fusion.48
  92.4 0.0 all-gather.3.cloned.1.call-done
  92.4 1.8 fusion.47
  94.2 0.5 fusion.51
  94.7 0.7 fusion.15
  95.4 0.7 convolution_convert_fusion.2
  96.1 0.5 convolution_convert_fusion.3
  96.6 0.2 copy.49
  96.8 0.2 copy.50
  97.0 0.5 convolution_convert_fusion.1
  97.4 0.5 convolution_convert_fusion
  97.9 1.6 pad_maximum_fusion
  99.5 0.0 reduce-scatter.2.cloned.1.call-update
  99.5 0.1 pad_maximum_fusion.1
  99.6 11.8 %all_to_all.37 = bf16[4,2,64,768]{3,2,1,0:T(8,128)(2,1)S(1)} all-to-all(bf16[4,2,64,768]{3,2,1,0:T(8,128)(2,1)S(1)} %pad_maximum_fusion.1), channel_id=1, replica_groups=mesh['x'=4,'y'=4,'z'=32,'c'=2] {'y'}, dimensions={0} | all-to-all | bytes 1572864 | tf_op jit(solution)/shard_map/all_to_all | solution.py:25
  111.4 0.1 reduce_sum.74
  111.5 0.2 copy.45
  111.7 45.4 %all_to_all.38 = bf16[64,2,768]{2,1,0:T(2,128)(2,1)S(1)} all-to-all(bf16[64,2,768]{2,1,0:T(2,128)(2,1)S(1)} %copy.45), channel_id=1, replica_groups=mesh['x'=4,'y'=4,'z'=32,'c'=2] {'z','c'}, dimensions={0} | all-to-all | bytes 393216 | tf_op jit(solution)/shard_map/all_to_all | solution.py:25
  157.2 0.3 fusion.49
  157.4 0.2 convolution_bitcast_fusion
  157.7 0.3 multiply_reduce_fusion.1
  157.9 0.1 add_convert_fusion
  158.0 0.2 convolution_convert_fusion.4
  158.3 13.8 %all_to_all.39 = bf16[32,2,768]{2,1,0:T(2,128)(2,1)S(1)} all-to-all(bf16[32,2,768]{2,1,0:T(2,128)(2,1)S(1)} %reshape.39), channel_id=1, replica_groups=mesh['x'=4,'y'=4,'z'=32,'c'=2] {'x','y','c'}, dimensions={0} | all-to-all | bytes 196608 | tf_op jit(solution)/shard_map/all_to_all | solution.py:25
  172.1 0.1 reduce_sum.77
  172.2 0.7 broadcast_in_dim.12
  172.9 3.9 %all-to-all-start.5 = ((bf16[32,2,768]{2,1,0:T(2,128)(2,1)}), bf16[32,2,768]{2,1,0:T(2,128)(2,1)S(1)}, u32[]{:S(2)}, u32[]{:S(2)}) async-start(bf16[32,2,768]{2,1,0:T(2,128)(2,1)} %broadcast_in_dim.12), calls=%async_computation.5 | async-start | bytes 196608 | tf_op jit(solution)/shard_map/all_to_all | solution.py:25
  176.7 0.3 fusion.52
  177.0 27.6 %all-to-all-done.5 = bf16[32,2,768]{2,1,0:T(2,128)(2,1)S(1)} async-done(((bf16[32,2,768]{2,1,0:T(2,128)(2,1)}), bf16[32,2,768]{2,1,0:T(2,128)(2,1)S(1)}, u32[]{:S(2)}, u32[]{:S(2)}) %all-to-all-start.5) | async-done | bytes 98336 | tf_op jit(solution)/shard_map/all_to_all | solution.py:25
  204.6 0.1 reduce_sum.78
  204.7 0.7 broadcast_in_dim.13
  205.4 5.3 %all-to-all-start.6 = ((bf16[32,2,768]{2,1,0:T(2,128)(2,1)}), bf16[32,2,768]{2,1,0:T(2,128)(2,1)S(1)}, u32[]{:S(2)}, u32[]{:S(2)}) async-start(bf16[32,2,768]{2,1,0:T(2,128)(2,1)} %broadcast_in_dim.13), calls=%async_computation.6 | async-start | bytes 196608 | tf_op jit(solution)/shard_map/all_to_all | solution.py:25
  210.7 1.1 fusion.1
  211.8 6.5 %all-to-all-done.6 = bf16[32,2,768]{2,1,0:T(2,128)(2,1)S(1)} async-done(((bf16[32,2,768]{2,1,0:T(2,128)(2,1)}), bf16[32,2,768]{2,1,0:T(2,128)(2,1)S(1)}, u32[]{:S(2)}, u32[]{:S(2)}) %all-to-all-start.6) | async-done | bytes 98336 | tf_op jit(solution)/shard_map/all_to_all | solution.py:25
  218.3 0.7 reshape.40
  219.0 0.0 reduce-scatter.2.cloned.1.call-done
  219.0 0.0 copy-start.1
  219.0 1.2 convert_element_type.68
  220.2 0.9 slice_bitcast_fusion
  221.1 0.0 copy-done.1
  221.1 0.9 slice.64
  (6 shorter events, 0.2 us)
Async XLA Ops:
  7.2 2.1 copy-start
  7.2 2.1 copy-start.2
  7.2 2.7 %copy-start.3 = (bf16[1,196,768]{2,1,0:T(8,128)(2,1)S(1)}, bf16[1,196,768]{2,1,0:T(8,128)(2,1)}, u32[]{:S(2)}) copy-start(bf16[1,196,768]{2,1,0:T(8,128)(2,1)} %param.9) | copy-start | bytes 903172
  7.2 85.2 %all-gather.3.cloned.1.call-start = ((), (), s32[]{:S(2)}) async-start(), calls=%async_computation.9 | async-start | bytes 2949120 | tf_op jit(solution)/shard_map/all_gather | solution.py:52
  9.2 209.8 %reduce-scatter.2.cloned.1.call-start = ((), (), s32[]{:S(2)}) async-start(), calls=%async_computation.8 | async-start | bytes 2949120 | tf_op jit(solution)/shard_map/reduce_scatter | solution.py:86
  172.9 31.7 %all-to-all-start.5 = ((bf16[32,2,768]{2,1,0:T(2,128)(2,1)}), bf16[32,2,768]{2,1,0:T(2,128)(2,1)S(1)}, u32[]{:S(2)}, u32[]{:S(2)}) async-start(bf16[32,2,768]{2,1,0:T(2,128)(2,1)} %broadcast_in_dim.12), calls=%async_computation.5 | async-start | bytes 196608 | tf_op jit(solution)/shard_map/all_to_all | solution.py:25
  205.4 12.9 %all-to-all-start.6 = ((bf16[32,2,768]{2,1,0:T(2,128)(2,1)}), bf16[32,2,768]{2,1,0:T(2,128)(2,1)S(1)}, u32[]{:S(2)}, u32[]{:S(2)}) async-start(bf16[32,2,768]{2,1,0:T(2,128)(2,1)} %broadcast_in_dim.13), calls=%async_computation.6 | async-start | bytes 196608 | tf_op jit(solution)/shard_map/all_to_all | solution.py:25
  219.0 2.1 copy-start.1
Sparse Core Ops, SparseCore 0:
  11.3 59.2 all-gather.2
  99.6 31.6 reduce-scatter.1

commit v2 on v1

--- a/solution.py
+++ b/solution.py
@@ -2,23 +2,14 @@
 import jax.numpy as jnp
 import numpy as np
 from jax import lax
+from jax.experimental import pallas as pl
+from jax.experimental.pallas import tpu as pltpu
 from jax.sharding import Mesh
 from jax.sharding import PartitionSpec as P
 
 BF = jnp.bfloat16
 F32 = jnp.float32
 ALL = ("x", "y", "z", "c")
-
-
-def gelu_exact(value):
-    return 0.5 * value * (1.0 + jax.scipy.special.erf(value * 0.7071067811865476))
-
-
-def gelu_slope(value):
-    return (
-        0.5 * (1.0 + jax.scipy.special.erf(value * 0.7071067811865476))
-        + value * jnp.exp(-0.5 * value * value) * 0.3989422804014327
-    )
 
 
 def exchange(parts, axes):
@@ -31,6 +22,72 @@
 
 def dot(a, b, dims):
     return lax.dot_general(a, b, (dims, ((), ())), preferred_element_type=F32)
+
+
+def expert_kernel(rows_ref, first_ref, second_ref, partial_ref, act_ref, pre_ref, out_sum, in_sum):
+    step = pl.program_id(0)
+    count, width = out_sum.shape
+    rows_in = rows_ref[:, 0].reshape(count, width)
+    rows_grad = rows_ref[:, 1].reshape(count, width)
+    first, second = first_ref[0], second_ref[0]
+    hidden = dot(rows_in, first, ((1,), (1,)))
+    act_grad = dot(rows_grad, second, ((1,), (1,)))
+    cdf = 0.5 * (1.0 + lax.erf(hidden * 0.7071067811865476))
+    slope = cdf + hidden * jnp.exp(-0.5 * hidden * hidden) * 0.3989422804014327
+    act = (hidden * cdf).astype(BF)
+    pre_grad = (act_grad * slope).astype(BF)
+    act_ref[0] = act
+    pre_ref[0] = pre_grad
+    out_part = dot(act, second, ((1,), (0,)))
+    in_part = dot(pre_grad, first, ((1,), (0,)))
+
+    @pl.when(step == 0)
+    def _():
+        out_sum[...] = out_part
+        in_sum[...] = in_part
+
+    @pl.when(step > 0)
+    def _():
+        out_sum[...] += out_part
+        in_sum[...] += in_part
+
+    @pl.when(step == pl.num_programs(0) - 1)
+    def _():
+        shape = partial_ref.shape[:1] + partial_ref.shape[2:]
+        partial_ref[:, 0] = out_sum[...].astype(BF).reshape(shape)
+        partial_ref[:, 1] = in_sum[...].astype(BF).reshape(shape)
+
+
+def expert_parts(rows, first, second):
+    ny, _, images, width = rows.shape
+    nx, block, _ = first.shape
+    count = ny * images
+    return pl.pallas_call(
+        expert_kernel,
+        grid=(nx,),
+        in_specs=[
+            pl.BlockSpec(rows.shape, lambda i: (0, 0, 0, 0)),
+            pl.BlockSpec((1, block, width), lambda i: (i, 0, 0)),
+            pl.BlockSpec((1, block, width), lambda i: (i, 0, 0)),
+        ],
+        out_specs=[
+            pl.BlockSpec(rows.shape, lambda i: (0, 0, 0, 0)),
+            pl.BlockSpec((1, count, block), lambda i: (i, 0, 0)),
+            pl.BlockSpec((1, count, block), lambda i: (i, 0, 0)),
+        ],
+        out_shape=[
+            jax.ShapeDtypeStruct(rows.shape, BF),
+            jax.ShapeDtypeStruct((nx, count, block), BF),
+            jax.ShapeDtypeStruct((nx, count, block), BF),
+        ],
+        scratch_shapes=[pltpu.VMEM((count, width), F32), pltpu.VMEM((count, width), F32)],
+        compiler_params=pltpu.CompilerParams(vmem_limit_bytes=40 * 1024 * 1024),
+        cost_estimate=pl.CostEstimate(
+            flops=8 * nx * count * block * width,
+            bytes_accessed=4 * rows.size + 4 * first.size + 4 * nx * count * block,
+            transcendentals=2 * nx * count * block,
+        ),
+    )(rows, first, second)
 
 
 def sum_of_all(local, nx, ny, nz, nc):
@@ -46,12 +103,9 @@
     tok, og = tokens[0], out_grad[0]
     width = tok.shape[1]
     experts = nz * nc
-    block = w_in.shape[2]
 
-    weights = jnp.concatenate([w_in[0].T, w_out[0]], axis=0)
-    gathered = lax.all_gather(weights, "x", axis=0, tiled=False)
-    first = gathered[:, :block].reshape(nx * block, width)
-    second = gathered[:, block:].reshape(nx * block, width)
+    first = lax.all_gather(w_in[0].T, "x", axis=0, tiled=False)
+    second = lax.all_gather(w_out[0], "x", axis=0, tiled=False)
 
     logits = jnp.dot(tok, router, preferred_element_type=F32)
     dispatch = jax.nn.softmax(logits, axis=0)
@@ -64,26 +118,20 @@
     mine = exchange(sent, ("z", "c"))
     pair = jnp.stack([mine[:, 0], mine[:, 1]], axis=0)
     rows = spread(pair, "y", ny)
+
+    partial, act, pre_grad = expert_parts(rows, first, second)
+    parts_of_mine = exchange(partial, "y")
     rows_in = rows[:, 0].reshape(ny * experts, width)
     rows_grad = rows[:, 1].reshape(ny * experts, width)
+    out_part = jnp.einsum("xrf,rd->xfd", act, rows_grad, preferred_element_type=F32)
+    in_part = jnp.einsum("xrf,rd->xfd", pre_grad, rows_in, preferred_element_type=F32)
+    parts_of_mine, out_part, in_part = lax.optimization_barrier((parts_of_mine, out_part, in_part))
+    w_in_grad = lax.psum_scatter(in_part, "x", scatter_dimension=0, tiled=False)
+    w_out_grad = lax.psum_scatter(out_part, "x", scatter_dimension=0, tiled=False)
 
-    hidden = dot(rows_in, first, ((1,), (1,)))
-    act = gelu_exact(hidden).astype(BF)
-    act_grad = dot(rows_grad, second, ((1,), (1,)))
-    pre_grad = (act_grad * gelu_slope(hidden)).astype(BF)
-    partial_out = dot(act, second, ((1,), (0,))).astype(BF)
-    partial_in = dot(pre_grad, first, ((1,), (0,))).astype(BF)
-    partial = jnp.stack(
-        [partial_out.reshape(ny, experts, width), partial_in.reshape(ny, experts, width)], axis=1
-    )
-    summed = exchange(partial, "y").astype(F32).sum(axis=0).astype(BF)
+    summed = parts_of_mine.astype(F32).sum(axis=0).astype(BF)
     back = exchange(jnp.stack([summed[0], summed[1]], axis=1), ("z", "c"))
     expert_out, slot_in_grad = back[:, 0], back[:, 1]
-
-    out_part = dot(act, rows_grad, ((0,), (0,))).reshape(nx, block, width)
-    in_part = dot(pre_grad, rows_in, ((0,), (0,))).reshape(nx, block, width)
-    parts = jnp.concatenate([in_part, out_part], axis=1)
-    grads = lax.psum_scatter(parts.astype(BF), "x", scatter_dimension=0, tiled=False).astype(F32)
 
     combine_dot = dot(og, expert_out, ((1,), (1,)))
     combine_part = combine * (combine_dot - jnp.sum(combine * combine_dot, axis=1, keepdims=True))
@@ -97,7 +145,7 @@
     token_grad = dot(logit_grad, router, ((1,), (1,))) + dot(
         dispatch_b, slot_in_grad, ((1,), (0,))
     )
-    return token_grad.astype(BF)[None], router_grad, grads[:block].T[None], grads[block:][None]
+    return token_grad.astype(BF)[None], router_grad, w_in_grad.T[None], w_out_grad[None]
 
 
 def solution(mesh):

time: 229 us -> 259 us (1.13)
  blocking collectives: 152 us -> 75.6 us
  waiting for transfers between devices: 34.1 us -> 99.7 us
  starting transfers between devices: 9.27 us -> 47.9 us
  other arithmetic: 5.52 us -> 0.7 us
  Pallas kernels: 0 us -> 4.39 us
    all_to_all x5 -> x2, blocking collectives: 152 us -> 75.6 us  [exchange(): return lax.all_to_all(parts, axes, split_axis=0, concat_axis=0, tiled=True)]
    all_to_all x2 -> x5, waiting for transfers between devices: 34.1 us -> 76.1 us  [exchange(): return lax.all_to_all(parts, axes, split_axis=0, concat_axis=0, tiled=True)]
    all_to_all x2 -> x5, starting transfers between devices: 9.19 us -> 47.8 us  [exchange(): return lax.all_to_all(parts, axes, split_axis=0, concat_axis=0, tiled=True)]
    all_gather x1 -> x2, waiting for transfers between devices: 0.02 us -> 21.7 us  [the longest x1 21.7 us: per_device(): second = lax.all_gather(w_out[0], 'x', axis=0, tiled=False)]
    pallas_call x0 -> x1, Pallas kernels: none -> 4.39 us  [expert_parts(): pl.pallas_call(expert_kernel, grid=(nx,), in_specs=[pl.BlockSpec(rows.sha...]
    dot_general x0 -> x2, matrix products: none -> 3.93 us  [the longest x1 1.97 us: per_device(): jnp.einsum('xrf,rd->xfd', act, rows_grad, preferred_element_type=F32)]
    concatenate x2 -> x0, other arithmetic: 3.53 us -> none  [the longest x1 1.96 us: per_device(): weights = jnp.concatenate([w_in[0].T, w_out[0]], axis=0)]
    unnamed x8 -> x10, local copies, waits for them, and re-layouts: 0.02 us -> 2.79 us
  transfers between devices with their start and end apart: 4 -> 9, of which waited for: 2 -> 5; matrix products, arithmetic and copies ran while one was open for 3% -> 5% of each run, Pallas kernels for 0% -> 0%
where the time goes in v2:
time: 259 us; the launch traced here: 258 us
  waiting for transfers between devices  99.7 us (38%)
  blocking collectives  75.6 us (29%)
  starting transfers between devices  47.9 us (18%)
  between operations  13.9 us (5%)
  matrix products  8.55 us (3%)
  local copies, waits for them, and re-layouts  7.61 us (3%)
  Pallas kernels  4.39 us (2%)
    all_to_all x5, waiting for transfers between devices, exchange(): return lax.all_to_all(parts, axes, split_axis=0, concat_axis=0, tiled=True)  76.1 us
    all_to_all x2, blocking collectives, exchange(): return lax.all_to_all(parts, axes, split_axis=0, concat_axis=0, tiled=True)  75.6 us
    all_to_all x5, starting transfers between devices, exchange(): return lax.all_to_all(parts, axes, split_axis=0, concat_axis=0, tiled=True)  47.8 us
    all_gather x1, waiting for transfers between devices, per_device(): second = lax.all_gather(w_out[0], 'x', axis=0, tiled=False)  21.7 us
  transfers between devices with their start and end apart: 9, of which 5 were waited for; matrix products, arithmetic and copies ran while one was open for 5% of the time, Pallas kernels for 0%

profile of v2, /device:TPU:1, one launch (start us, length us, event | category | flops | bytes accessed | tf_op | source)
XLA Modules:
  0.0 258.5 jit_solution(5304443903301524021)
XLA Ops:
  7.2 0.0 copy-start
  7.2 0.0 all-gather.6.cloned.1.call-start
  7.2 0.7 all-gather.6.cloned.1.call-update
  7.9 0.2 copy-done
  8.1 1.2 fusion.21
  9.4 0.2 fusion.14
  9.6 1.1 fusion.3
  10.7 0.2 fusion.2
  11.0 0.9 copy.32
  11.9 30.4 %all-to-all-start = ((bf16[64,2,768]{2,1,0:T(2,128)(2,1)}), bf16[64,2,768]{2,1,0:T(2,128)(2,1)S(1)}, u32[]{:S(2)}, u32[]{:S(2)}) async-start(bf16[64,2,768]{2,1,0:T(2,128)(2,1)} %copy.32), calls=%async_computation | async-start | bytes 393216 | tf_op jit(solution)/shard_map/all_to_all | solution.py:16
  42.3 0.0 all-gather.4.cloned.1.call-start
  42.3 0.7 all-gather.4.cloned.1.call-update
  43.1 35.9 %all-to-all-done = bf16[64,2,768]{2,1,0:T(2,128)(2,1)S(1)} async-done(((bf16[64,2,768]{2,1,0:T(2,128)(2,1)}), bf16[64,2,768]{2,1,0:T(2,128)(2,1)S(1)}, u32[]{:S(2)}, u32[]{:S(2)}) %all-to-all-start) | async-done | bytes 196640 | tf_op jit(solution)/shard_map/all_to_all | solution.py:16
  78.9 0.3 fusion.24
  79.3 0.9 broadcast_in_dim.10
  80.2 4.2 %all-to-all-start.1 = ((bf16[4,2,64,768]{3,2,1,0:T(8,128)(2,1)}), bf16[4,2,64,768]{3,2,1,0:T(8,128)(2,1)S(1)}, u32[]{:S(2)}, u32[]{:S(2)}) async-start(bf16[4,2,64,768]{3,2,1,0:T(8,128)(2,1)} %broadcast_in_dim.10), calls=%async_computation.1 | async-start | bytes 1572864 | tf_op jit(solution)/shard_map/all_to_all | solution.py:16
  84.4 0.0 all-gather.6.cloned.1.call-done
  84.4 21.7 %all-gather.4.cloned.1.call-done.second_ref = bf16[4,192,768]{2,1,0:T(8,128)(2,1)} async-done(((bf16[1,192,768]{2,1,0:T(8,128)(2,1)}), bf16[4,192,768]{2,1,0:T(8,128)(2,1)}) %all-gather.4.cloned.1.call-update) | async-done | bytes 1179664 | tf_op jit(solution)/shard_map/all_gather | solution.py:108
  106.1 0.0 all-to-all-done.1.rows_ref
  106.1 0.0 copy-start.1
  106.1 1.3 copy-done.1
  107.4 0.0 copy-start.2
  107.4 1.3 copy-done.2
  108.7 4.4 %shard_map.84 = (bf16[4,2,64,768]{3,2,1,0:T(8,128)(2,1)}, bf16[4,256,192]{2,1,0:T(8,128)(2,1)S(1)}, bf16[4,256,192]{2,1,0:T(8,128)(2,1)S(1)}) custom-call(bf16[4,2,64,768]{3,2,1,0:T(8,128)(2,1)S(1)} %all-to-all-done.1.rows_ref, bf16[4,192,768]{2,1,0:T(8,128)(2,1)S(1)} %bitcast.69, bf16[4,192,768]{2,1,0:T(8,128)(2,1)S(1)} %copy-done.2), custom_call_target="tpu_custom_call" | custom-call | flops 1207959552 | bytes 4718592 | tf_op jit(solution)/shard_map/pallas_call | solution.py:65
  113.1 4.0 %all-to-all-start.2 = ((bf16[4,2,64,768]{3,2,1,0:T(8,128)(2,1)}), bf16[4,2,64,768]{3,2,1,0:T(8,128)(2,1)S(1)}, u32[]{:S(2)}, u32[]{:S(2)}) async-start(bf16[4,2,64,768]{3,2,1,0:T(8,128)(2,1)} %get-tuple-element.10), calls=%async_computation.2 | async-start | bytes 1572864 | tf_op jit(solution)/shard_map/all_to_all | solution.py:16
  117.1 0.0 reduce-scatter.3.cloned.1.call-start
  117.1 0.1 fusion.22
  117.1 2.0 fusion.25
  119.1 2.0 fusion.26
  121.1 6.1 %all-to-all-done.2 = bf16[4,2,64,768]{3,2,1,0:T(8,128)(2,1)S(1)} async-done(((bf16[4,2,64,768]{3,2,1,0:T(8,128)(2,1)}), bf16[4,2,64,768]{3,2,1,0:T(8,128)(2,1)S(1)}, u32[]{:S(2)}, u32[]{:S(2)}) %all-to-all-start.2) | async-done | bytes 786464 | tf_op jit(solution)/shard_map/all_to_all | solution.py:16
  127.2 0.0 reduce-scatter.3.cloned.1.call-update
  127.2 0.0 reduce-scatter.5.cloned.1.call-start
  127.3 0.5 reduce-scatter.5.cloned.1.call-update
  127.8 0.0 copy-start.4
  127.8 0.1 reduce_sum.74
  128.0 0.0 copy-start.3
  128.0 0.2 copy.37
  128.2 62.7 %all_to_all.35 = bf16[64,2,768]{2,1,0:T(2,128)(2,1)S(1)} all-to-all(bf16[64,2,768]{2,1,0:T(2,128)(2,1)S(1)} %copy.37), channel_id=1, replica_groups=mesh['x'=4,'y'=4,'z'=32,'c'=2] {'z','c'}, dimensions={0} | all-to-all | bytes 393216 | tf_op jit(solution)/shard_map/all_to_all | solution.py:16
  190.9 0.3 fusion.23
  191.2 0.2 convolution_bitcast_fusion
  191.4 0.0 copy-done.4
  191.4 0.3 multiply_reduce_fusion.1
  191.7 0.1 add_convert_fusion
  191.8 0.2 convolution_convert_fusion
  192.0 13.0 %all_to_all.36 = bf16[32,2,768]{2,1,0:T(2,128)(2,1)S(1)} all-to-all(bf16[32,2,768]{2,1,0:T(2,128)(2,1)S(1)} %reshape.23), channel_id=1, replica_groups=mesh['x'=4,'y'=4,'z'=32,'c'=2] {'x','y','c'}, dimensions={0} | all-to-all | bytes 196608 | tf_op jit(solution)/shard_map/all_to_all | solution.py:16
  205.0 0.1 reduce_sum.77
  205.1 0.7 broadcast_in_dim.12
  205.8 3.9 %all-to-all-start.5 = ((bf16[32,2,768]{2,1,0:T(2,128)(2,1)}), bf16[32,2,768]{2,1,0:T(2,128)(2,1)S(1)}, u32[]{:S(2)}, u32[]{:S(2)}) async-start(bf16[32,2,768]{2,1,0:T(2,128)(2,1)} %broadcast_in_dim.12), calls=%async_computation.5 | async-start | bytes 196608 | tf_op jit(solution)/shard_map/all_to_all | solution.py:16
  209.6 0.0 copy-done.3
  209.7 0.3 fusion.27
  209.9 27.6 %all-to-all-done.5 = bf16[32,2,768]{2,1,0:T(2,128)(2,1)S(1)} async-done(((bf16[32,2,768]{2,1,0:T(2,128)(2,1)}), bf16[32,2,768]{2,1,0:T(2,128)(2,1)S(1)}, u32[]{:S(2)}, u32[]{:S(2)}) %all-to-all-start.5) | async-done | bytes 98336 | tf_op jit(solution)/shard_map/all_to_all | solution.py:16
  237.5 0.1 reduce_sum.78
  237.6 0.7 broadcast_in_dim.13
  238.3 5.3 %all-to-all-start.6 = ((bf16[32,2,768]{2,1,0:T(2,128)(2,1)}), bf16[32,2,768]{2,1,0:T(2,128)(2,1)S(1)}, u32[]{:S(2)}, u32[]{:S(2)}) async-start(bf16[32,2,768]{2,1,0:T(2,128)(2,1)} %broadcast_in_dim.13), calls=%async_computation.6 | async-start | bytes 196608 | tf_op jit(solution)/shard_map/all_to_all | solution.py:16
  243.6 1.1 fusion.1
  244.7 6.5 %all-to-all-done.6 = bf16[32,2,768]{2,1,0:T(2,128)(2,1)S(1)} async-done(((bf16[32,2,768]{2,1,0:T(2,128)(2,1)}), bf16[32,2,768]{2,1,0:T(2,128)(2,1)S(1)}, u32[]{:S(2)}, u32[]{:S(2)}) %all-to-all-start.6) | async-done | bytes 98336 | tf_op jit(solution)/shard_map/all_to_all | solution.py:16
  251.2 0.7 reshape.24
  251.9 0.0 reduce-scatter.3.cloned.1.call-done
  251.9 0.0 reduce-scatter.5.cloned.1.call-done
  (6 shorter events, 0.2 us)
Async XLA Ops:
  7.2 1.0 copy-start
  7.2 77.2 %all-gather.6.cloned.1.call-start = ((), (), s32[]{:S(2)}) async-start(), calls=%async_computation.12 | async-start | bytes 1474560 | tf_op jit(solution)/shard_map/all_gather | solution.py:107
  11.9 67.1 %all-to-all-start = ((bf16[64,2,768]{2,1,0:T(2,128)(2,1)}), bf16[64,2,768]{2,1,0:T(2,128)(2,1)S(1)}, u32[]{:S(2)}, u32[]{:S(2)}) async-start(bf16[64,2,768]{2,1,0:T(2,128)(2,1)} %copy.32), calls=%async_computation | async-start | bytes 393216 | tf_op jit(solution)/shard_map/all_to_all | solution.py:16
  42.3 63.8 %all-gather.4.cloned.1.call-start = ((), (), s32[]{:S(2)}) async-start(), calls=%async_computation.9 | async-start | bytes 1474560 | tf_op jit(solution)/shard_map/all_gather | solution.py:108
  80.2 25.9 %all-to-all-start.1 = ((bf16[4,2,64,768]{3,2,1,0:T(8,128)(2,1)}), bf16[4,2,64,768]{3,2,1,0:T(8,128)(2,1)S(1)}, u32[]{:S(2)}, u32[]{:S(2)}) async-start(bf16[4,2,64,768]{3,2,1,0:T(8,128)(2,1)} %broadcast_in_dim.10), calls=%async_computation.1 | async-start | bytes 1572864 | tf_op jit(solution)/shard_map/all_to_all | solution.py:16
  106.1 1.3 copy-start.1
  107.4 1.3 copy-start.2
  113.1 14.1 %all-to-all-start.2 = ((bf16[4,2,64,768]{3,2,1,0:T(8,128)(2,1)}), bf16[4,2,64,768]{3,2,1,0:T(8,128)(2,1)S(1)}, u32[]{:S(2)}, u32[]{:S(2)}) async-start(bf16[4,2,64,768]{3,2,1,0:T(8,128)(2,1)} %get-tuple-element.10), calls=%async_computation.2 | async-start | bytes 1572864 | tf_op jit(solution)/shard_map/all_to_all | solution.py:16
  117.1 134.8 %reduce-scatter.3.cloned.1.call-start = ((), (), s32[]{:S(2)}) async-start(), calls=%async_computation.10 | async-start | bytes 2949120 | tf_op jit(solution)/shard_map/reduce_scatter | solution.py:129
  127.2 124.7 %reduce-scatter.5.cloned.1.call-start = ((), (), s32[]{:S(2)}) async-start(), calls=%async_computation.11 | async-start | bytes 2949120 | tf_op jit(solution)/shard_map/reduce_scatter | solution.py:130
  127.8 63.6 %copy-start.4 = (bf16[1,196,768]{2,1,0:T(8,128)(2,1)S(1)}, bf16[1,196,768]{2,1,0:T(8,128)(2,1)}, u32[]{:S(2)}) copy-start(bf16[1,196,768]{2,1,0:T(8,128)(2,1)} %param.9) | copy-start | bytes 903172
  128.0 81.7 %copy-start.3 = (bf16[768,64]{0,1:T(8,128)(2,1)S(1)}, bf16[768,64]{0,1:T(8,128)(2,1)}, u32[]{:S(2)}) copy-start(bf16[768,64]{0,1:T(8,128)(2,1)} %param.6) | copy-start | bytes 294916
  205.8 31.7 %all-to-all-start.5 = ((bf16[32,2,768]{2,1,0:T(2,128)(2,1)}), bf16[32,2,768]{2,1,0:T(2,128)(2,1)S(1)}, u32[]{:S(2)}, u32[]{:S(2)}) async-start(bf16[32,2,768]{2,1,0:T(2,128)(2,1)} %broadcast_in_dim.12), calls=%async_computation.5 | async-start | bytes 196608 | tf_op jit(solution)/shard_map/all_to_all | solution.py:16
  238.3 12.9 %all-to-all-start.6 = ((bf16[32,2,768]{2,1,0:T(2,128)(2,1)}), bf16[32,2,768]{2,1,0:T(2,128)(2,1)S(1)}, u32[]{:S(2)}, u32[]{:S(2)}) async-start(bf16[32,2,768]{2,1,0:T(2,128)(2,1)} %broadcast_in_dim.13), calls=%async_computation.6 | async-start | bytes 196608 | tf_op jit(solution)/shard_map/all_to_all | solution.py:16
Sparse Core Ops, SparseCore 0:
  10.7 49.6 all-gather.5
  63.0 43.0 all-gather.3
  127.3 51.0 reduce-scatter.2
  182.3 49.6 reduce-scatter.4

commit v3 on v2

--- a/solution.py
+++ b/solution.py
@@ -10,6 +10,7 @@
 BF = jnp.bfloat16
 F32 = jnp.float32
 ALL = ("x", "y", "z", "c")
+VMEM_BYTES = 60 * 1024 * 1024
 
 
 def exchange(parts, axes):
@@ -22,6 +23,60 @@
 
 def dot(a, b, dims):
     return lax.dot_general(a, b, (dims, ((), ())), preferred_element_type=F32)
+
+
+def front_kernel(
+    tok_ref, router_ref, grad_ref, first_ref, second_ref,
+    dispatch_ref, combine_ref, dispatch_b_ref, slots_ref, weights_ref, sems,
+):
+    block = first_ref.shape[0]
+    copies = [
+        pltpu.make_async_copy(first_ref, weights_ref.at[pl.ds(0, block)], sems.at[0]),
+        pltpu.make_async_copy(second_ref, weights_ref.at[pl.ds(block, block)], sems.at[1]),
+    ]
+    for copy in copies:
+        copy.start()
+    tok = tok_ref[...]
+    logits = dot(tok, router_ref[...], ((1,), (1,)))
+    up = jnp.exp(logits - jnp.max(logits, axis=0, keepdims=True))
+    dispatch = up / jnp.sum(up, axis=0, keepdims=True)
+    across = jnp.exp(logits - jnp.max(logits, axis=1, keepdims=True))
+    combine = across / jnp.sum(across, axis=1, keepdims=True)
+    dispatch_ref[...] = dispatch
+    combine_ref[...] = combine
+    dispatch_b = dispatch.astype(BF)
+    dispatch_b_ref[...] = dispatch_b
+    slots_ref[0] = dot(dispatch_b, tok, ((0,), (0,))).astype(BF)
+    slots_ref[1] = dot(combine.astype(BF), grad_ref[...], ((0,), (0,))).astype(BF)
+    for copy in copies:
+        copy.wait()
+
+
+def front(tok, router_t, og, first, second):
+    count, width = tok.shape
+    experts = router_t.shape[0]
+    block = first.shape[0]
+    whole = pl.BlockSpec(memory_space=pltpu.VMEM)
+    placed = pl.BlockSpec(memory_space=pl.ANY)
+    return pl.pallas_call(
+        front_kernel,
+        in_specs=[whole, whole, whole, placed, placed],
+        out_specs=[whole, whole, whole, whole, placed],
+        out_shape=[
+            jax.ShapeDtypeStruct((count, experts), F32),
+            jax.ShapeDtypeStruct((count, experts), F32),
+            jax.ShapeDtypeStruct((count, experts), BF),
+            jax.ShapeDtypeStruct((2, experts, width), BF),
+            jax.ShapeDtypeStruct((2 * block, width), BF),
+        ],
+        scratch_shapes=[pltpu.SemaphoreType.DMA((2,))],
+        compiler_params=pltpu.CompilerParams(vmem_limit_bytes=VMEM_BYTES),
+        cost_estimate=pl.CostEstimate(
+            flops=6 * count * width * experts,
+            bytes_accessed=4 * tok.size + 8 * first.size,
+            transcendentals=2 * count * experts,
+        ),
+    )(tok, router_t, og, first, second)
 
 
 def expert_kernel(rows_ref, first_ref, second_ref, partial_ref, act_ref, pre_ref, out_sum, in_sum):
@@ -58,9 +113,10 @@
         partial_ref[:, 1] = in_sum[...].astype(BF).reshape(shape)
 
 
-def expert_parts(rows, first, second):
+def expert_parts(rows, weights):
     ny, _, images, width = rows.shape
-    nx, block, _ = first.shape
+    nx, double, _ = weights.shape
+    block = double // 2
     count = ny * images
     return pl.pallas_call(
         expert_kernel,
@@ -68,7 +124,7 @@
         in_specs=[
             pl.BlockSpec(rows.shape, lambda i: (0, 0, 0, 0)),
             pl.BlockSpec((1, block, width), lambda i: (i, 0, 0)),
-            pl.BlockSpec((1, block, width), lambda i: (i, 0, 0)),
+            pl.BlockSpec((1, block, width), lambda i: (i, 1, 0)),
         ],
         out_specs=[
             pl.BlockSpec(rows.shape, lambda i: (0, 0, 0, 0)),
@@ -81,53 +137,63 @@
             jax.ShapeDtypeStruct((nx, count, block), BF),
         ],
         scratch_shapes=[pltpu.VMEM((count, width), F32), pltpu.VMEM((count, width), F32)],
-        compiler_params=pltpu.CompilerParams(vmem_limit_bytes=40 * 1024 * 1024),
+        compiler_params=pltpu.CompilerParams(vmem_limit_bytes=VMEM_BYTES),
         cost_estimate=pl.CostEstimate(
             flops=8 * nx * count * block * width,
-            bytes_accessed=4 * rows.size + 4 * first.size + 4 * nx * count * block,
+            bytes_accessed=4 * rows.size + 2 * weights.size + 4 * nx * count * block,
             transcendentals=2 * nx * count * block,
         ),
-    )(rows, first, second)
-
-
-def sum_of_all(local, nx, ny, nz, nc):
-    experts, width = local.shape
-    plane = nx * ny * nc
-    pieces = local.astype(BF).reshape(plane, experts // plane, width)
-    mine = exchange(pieces, ("x", "y", "c")).astype(F32).sum(axis=0).astype(BF)
-    total = spread(mine, "z", nz).astype(F32).sum(axis=0).astype(BF)
-    return spread(total, ("x", "y", "c"), plane).reshape(experts, width).astype(F32)
+    )(rows, weights, weights)
+
+
+def weight_kernel(rows_ref, act_ref, pre_ref, parts_ref):
+    ny, _, images, width = rows_ref.shape
+    block = act_ref.shape[2]
+    rows_in = rows_ref[:, 0].reshape(ny * images, width)
+    rows_grad = rows_ref[:, 1].reshape(ny * images, width)
+    parts_ref[0, :block] = dot(pre_ref[0], rows_in, ((0,), (0,))).astype(BF)
+    parts_ref[0, block:] = dot(act_ref[0], rows_grad, ((0,), (0,))).astype(BF)
+
+
+def weight_parts(rows, act, pre_grad):
+    nx, count, block = act.shape
+    width = rows.shape[3]
+    return pl.pallas_call(
+        weight_kernel,
+        grid=(nx,),
+        in_specs=[
+            pl.BlockSpec(rows.shape, lambda i: (0, 0, 0, 0)),
+            pl.BlockSpec((1, count, block), lambda i: (i, 0, 0)),
+            pl.BlockSpec((1, count, block), lambda i: (i, 0, 0)),
+        ],
+        out_specs=pl.BlockSpec((1, 2 * block, width), lambda i: (i, 0, 0)),
+        out_shape=jax.ShapeDtypeStruct((nx, 2 * block, width), BF),
+        compiler_params=pltpu.CompilerParams(vmem_limit_bytes=VMEM_BYTES),
+        cost_estimate=pl.CostEstimate(
+            flops=4 * nx * count * block * width,
+            bytes_accessed=2 * rows.size + 4 * act.size + 4 * nx * block * width,
+            transcendentals=0,
+        ),
+    )(rows, act, pre_grad)
 
 
 def per_device(nx, ny, nz, nc, tokens, router, w_in, w_out, out_grad):
     tok, og = tokens[0], out_grad[0]
     width = tok.shape[1]
     experts = nz * nc
-
-    first = lax.all_gather(w_in[0].T, "x", axis=0, tiled=False)
-    second = lax.all_gather(w_out[0], "x", axis=0, tiled=False)
-
-    logits = jnp.dot(tok, router, preferred_element_type=F32)
-    dispatch = jax.nn.softmax(logits, axis=0)
-    combine = jax.nn.softmax(logits, axis=1)
-    dispatch_b = dispatch.astype(BF)
-    combine_b = combine.astype(BF)
-    slots = dot(dispatch_b, tok, ((0,), (0,))).astype(BF)
-    slot_grad = dot(combine_b, og, ((0,), (0,))).astype(BF)
-    sent = jnp.stack([slots, slot_grad], axis=1)
-    mine = exchange(sent, ("z", "c"))
-    pair = jnp.stack([mine[:, 0], mine[:, 1]], axis=0)
-    rows = spread(pair, "y", ny)
-
-    partial, act, pre_grad = expert_parts(rows, first, second)
+    block = w_out.shape[1]
+    plane = nx * ny * nc
+
+    dispatch, combine, dispatch_b, slots, weights = front(tok, router.T, og, w_in[0].T, w_out[0])
+    gathered = lax.all_gather(weights, "x", axis=0, tiled=False)
+    mine = exchange(jnp.stack([slots[0], slots[1]], axis=1), ("z", "c"))
+    rows = spread(jnp.stack([mine[:, 0], mine[:, 1]], axis=0), "y", ny)
+
+    partial, act, pre_grad = expert_parts(rows, gathered)
     parts_of_mine = exchange(partial, "y")
-    rows_in = rows[:, 0].reshape(ny * experts, width)
-    rows_grad = rows[:, 1].reshape(ny * experts, width)
-    out_part = jnp.einsum("xrf,rd->xfd", act, rows_grad, preferred_element_type=F32)
-    in_part = jnp.einsum("xrf,rd->xfd", pre_grad, rows_in, preferred_element_type=F32)
-    parts_of_mine, out_part, in_part = lax.optimization_barrier((parts_of_mine, out_part, in_part))
-    w_in_grad = lax.psum_scatter(in_part, "x", scatter_dimension=0, tiled=False)
-    w_out_grad = lax.psum_scatter(out_part, "x", scatter_dimension=0, tiled=False)
+    parts = weight_parts(rows, act, pre_grad)
+    parts_of_mine, parts = lax.optimization_barrier((parts_of_mine, parts))
+    grads = lax.psum_scatter(parts, "x", scatter_dimension=0, tiled=False)
 
     summed = parts_of_mine.astype(F32).sum(axis=0).astype(BF)
     back = exchange(jnp.stack([summed[0], summed[1]], axis=1), ("z", "c"))
@@ -140,12 +206,24 @@
         dispatch_dot - jnp.sum(dispatch * dispatch_dot, axis=0, keepdims=True)
     )
     logit_grad = (combine_part + dispatch_part).astype(BF)
-    router_local = dot(logit_grad, tok, ((0,), (0,)))
-    router_grad = sum_of_all(router_local, nx, ny, nz, nc).T
+
+    local = dot(logit_grad, tok, ((0,), (0,))).astype(BF)
+    pieces = exchange(local.reshape(plane, experts // plane, width), ("x", "y", "c"))
+    piece = pieces.astype(F32).sum(axis=0).astype(BF)
+    piece, grads, logit_grad = lax.optimization_barrier((piece, grads, logit_grad))
+    along_z = spread(piece, "z", nz)
+    w_in_grad = grads[:block].astype(F32)
+    w_out_grad = grads[block:].astype(F32)
     token_grad = dot(logit_grad, router, ((1,), (1,))) + dot(
         dispatch_b, slot_in_grad, ((1,), (0,))
     )
-    return token_grad.astype(BF)[None], router_grad, w_in_grad.T[None], w_out_grad[None]
+    token_grad = token_grad.astype(BF)
+    along_z, w_in_grad, w_out_grad, token_grad = lax.optimization_barrier(
+        (along_z, w_in_grad, w_out_grad, token_grad)
+    )
+    total = along_z.astype(F32).sum(axis=0).astype(BF)
+    router_grad = spread(total, ("x", "y", "c"), plane).reshape(experts, width).astype(F32).T
+    return token_grad[None], router_grad, w_in_grad.T[None], w_out_grad[None]
 
 
 def solution(mesh):

time: 259 us -> 244 us (0.942)
  blocking collectives: 75.6 us -> 153 us
  waiting for transfers between devices: 99.7 us -> 30.3 us
  starting transfers between devices: 47.9 us -> 7.43 us
  Pallas kernels: 4.39 us -> 31.6 us
  matrix products: 8.55 us -> 1.93 us
  local copies, waits for them, and re-layouts: 7.61 us -> 3.56 us
    all_to_all x2 -> x5, blocking collectives: 75.6 us -> 153 us  [exchange(): return lax.all_to_all(parts, axes, split_axis=0, concat_axis=0, tiled=True)]
    all_to_all x5 -> x2, waiting for transfers between devices: 76.1 us -> 30.2 us  [exchange(): return lax.all_to_all(parts, axes, split_axis=0, concat_axis=0, tiled=True)]
    all_to_all x5 -> x2, starting transfers between devices: 47.8 us -> 7.35 us  [exchange(): return lax.all_to_all(parts, axes, split_axis=0, concat_axis=0, tiled=True)]
    pallas_call x0 -> x2, Pallas kernels: none -> 25.5 us  [the longest x1 20.9 us: front(): pl.pallas_call(front_kernel, in_specs=[whole, whole, whole, placed, place...]
    all_gather x2 -> x1, waiting for transfers between devices: 21.7 us -> 0.01 us  [per_device(): gathered = lax.all_gather(weights, 'x', axis=0, tiled=False)]
    dot_general x3 -> x0, matrix products: 5.17 us -> none  [the longest x1 1.97 us: per_device(): jnp.einsum('xrf,rd->xfd', act, rows_grad, preferred_element_type=F32)]
    unnamed x10 -> x14, local copies, waits for them, and re-layouts: 2.79 us -> 0.03 us
  transfers between devices with their start and end apart: 9 -> 4, of which waited for: 5 -> 2; matrix products, arithmetic and copies ran while one was open for 5% -> 2% of each run, Pallas kernels for 0% -> 2%
where the time goes in v3:
time: 244 us
  blocking collectives  153 us (63%)
  Pallas kernels  31.6 us (13%)
  waiting for transfers between devices  30.3 us (12%)
  between operations  14.3 us (6%)
  starting transfers between devices  7.43 us (3%)
  local copies, waits for them, and re-layouts  3.56 us (1%)
    all_to_all x5, blocking collectives, exchange(): return lax.all_to_all(parts, axes, split_axis=0, concat_axis=0, tiled=True)  153 us
    all_to_all x2, waiting for transfers between devices, exchange(): return lax.all_to_all(parts, axes, split_axis=0, concat_axis=0, tiled=True)  30.2 us
    pallas_call x1, Pallas kernels, front(): pl.pallas_call(front_kernel, in_specs=[whole, whole, whole, placed, place...  20.9 us
    all_to_all x2, starting transfers between devices, exchange(): return lax.all_to_all(parts, axes, split_axis=0, concat_axis=0, tiled=True)  7.35 us
    pallas_call x1, Pallas kernels, expert_parts(): pl.pallas_call(expert_kernel, grid=(nx,), in_specs=[pl.BlockSpec(rows.sha...  6.13 us
  transfers between devices with their start and end apart: 4, of which 2 were waited for; matrix products, arithmetic and copies ran while one was open for 2% of the time, Pallas kernels for 2%

profile of v3, /device:TPU:1, one launch (start us, length us, event | category | flops | bytes accessed | tf_op | source)
XLA Modules:
  0.0 243.8 jit_solution(4117443643774528738)
XLA Ops:
  7.2 0.0 all-gather.3.cloned.1.call-start
  7.2 20.9 %shard_map.84 = (f32[196,64]{1,0:T(8,128)}, f32[196,64]{1,0:T(8,128)}, bf16[196,64]{1,0:T(8,128)(2,1)}, bf16[2,64,768]{2,1,0:T(8,128)(2,1)}, bf16[384,768]{1,0:T(8,128)(2,1)}) custom-call(bf16[196,768]{1,0:T(8,128)(2,1)} %bitcast.58, bf16[64,768]{1,0:T(8,128)(2,1)} %bitcast.63, bf16[196,768]{1,0:T(8,128)(2,1)} %bitcast.59, bf16[192,768]{1,0:T(8,128)(2,1)} %bitcast.65, ...), custom_call_target="tpu_custom_call" | custom-call | flops 57802752 | bytes 1781760 | tf_op jit(solution)/shard_map/pallas_call | solution.py:61
  28.1 0.0 all-gather.3.cloned.1.call-update
  28.1 1.0 slice_bitcast_fusion.3
  29.1 0.2 copy.16
  29.3 66.8 %all_to_all.35 = bf16[64,2,768]{2,1,0:T(2,128)(2,1)S(1)} all-to-all(bf16[64,2,768]{2,1,0:T(2,128)(2,1)S(1)} %copy.16), channel_id=1, replica_groups=mesh['x'=4,'y'=4,'z'=32,'c'=2] {'z','c'}, dimensions={0} | all-to-all | bytes 393216 | tf_op jit(solution)/shard_map/all_to_all | solution.py:17
  96.2 0.3 fusion.5
  96.5 0.1 broadcast_in_dim.12
  96.6 14.6 %all_to_all.36.rows_ref = bf16[4,2,64,768]{3,2,1,0:T(8,128)(2,1)} all-to-all(bf16[4,2,64,768]{3,2,1,0:T(8,128)(2,1)S(1)} %broadcast_in_dim.12), channel_id=1, replica_groups=mesh['x'=4,'y'=4,'z'=32,'c'=2] {'y'}, dimensions={0} | all-to-all | bytes 1572864 | tf_op jit(solution)/shard_map/all_to_all | solution.py:17
  111.2 0.0 all-gather.3.cloned.1.call-done
  111.2 6.1 %shard_map.85 = (bf16[4,2,64,768]{3,2,1,0:T(8,128)(2,1)}, bf16[4,256,192]{2,1,0:T(8,128)(2,1)}, bf16[4,256,192]{2,1,0:T(8,128)(2,1)}) custom-call(bf16[4,2,64,768]{3,2,1,0:T(8,128)(2,1)} %all_to_all.36.rows_ref, bf16[4,384,768]{2,1,0:T(8,128)(2,1)} %bitcast.56, bf16[4,384,768]{2,1,0:T(8,128)(2,1)} %bitcast.57), custom_call_target="tpu_custom_call" | custom-call | flops 1207959552 | bytes 4718592 | tf_op jit(solution)/shard_map/pallas_call | solution.py:121
  117.3 3.5 %all-to-all-start.2 = ((bf16[4,2,64,768]{3,2,1,0:T(8,128)(2,1)}), bf16[4,2,64,768]{3,2,1,0:T(8,128)(2,1)S(1)}, u32[]{:S(2)}, u32[]{:S(2)}) async-start(bf16[4,2,64,768]{3,2,1,0:T(8,128)(2,1)} %get-tuple-element.24), calls=%async_computation.2 | async-start | bytes 1572864 | tf_op jit(solution)/shard_map/all_to_all | solution.py:17
  120.8 0.0 reduce-scatter.2.cloned.1.call-start
  120.9 4.6 %shard_map.86 = bf16[4,384,768]{2,1,0:T(8,128)(2,1)} custom-call(bf16[4,2,64,768]{3,2,1,0:T(8,128)(2,1)} %all_to_all.36.rows_ref, bf16[4,256,192]{2,1,0:T(8,128)(2,1)} %get-tuple-element.25.act_ref, bf16[4,256,192]{2,1,0:T(8,128)(2,1)} %get-tuple-element.26.pre_ref), custom_call_target="tpu_custom_call" | custom-call | flops 603979776 | bytes 3932160 | tf_op jit(solution)/shard_map/pallas_call | solution.py:161
  125.5 0.0 copy-start.1
  125.5 0.0 copy-start.3
  125.5 4.6 %all-to-all-done.2 = bf16[4,2,64,768]{3,2,1,0:T(8,128)(2,1)S(1)} async-done(((bf16[4,2,64,768]{3,2,1,0:T(8,128)(2,1)}), bf16[4,2,64,768]{3,2,1,0:T(8,128)(2,1)S(1)}, u32[]{:S(2)}, u32[]{:S(2)}) %all-to-all-start.2) | async-done | bytes 786464 | tf_op jit(solution)/shard_map/all_to_all | solution.py:17
  130.1 0.0 reduce-scatter.2.cloned.1.call-update
  130.2 0.0 copy-start
  130.2 0.0 copy-start.4
  130.2 0.1 reduce_sum.54
  130.4 0.0 copy-start.5
  130.4 0.2 copy.19
  130.6 0.0 copy-start.6
  130.6 45.5 %all_to_all.37 = bf16[64,2,768]{2,1,0:T(2,128)(2,1)S(1)} all-to-all(bf16[64,2,768]{2,1,0:T(2,128)(2,1)S(1)} %copy.19), channel_id=1, replica_groups=mesh['x'=4,'y'=4,'z'=32,'c'=2] {'z','c'}, dimensions={0} | all-to-all | bytes 393216 | tf_op jit(solution)/shard_map/all_to_all | solution.py:17
  176.1 0.3 fusion.4
  176.4 0.0 copy-done.1
  176.4 0.0 copy-done.3
  176.4 0.3 multiply_reduce_fusion.1
  176.8 0.0 copy-done
  176.8 0.0 copy-done.4
  176.8 0.2 multiply_reduce_fusion
  177.0 0.1 add_convert_fusion
  177.1 0.2 convolution_convert_fusion
  177.3 0.1 reshape.19
  177.4 13.8 %all_to_all.38 = bf16[32,2,768]{2,1,0:T(2,128)(2,1)S(1)} all-to-all(bf16[32,2,768]{2,1,0:T(2,128)(2,1)S(1)} %reshape.19), channel_id=1, replica_groups=mesh['x'=4,'y'=4,'z'=32,'c'=2] {'x','y','c'}, dimensions={0} | all-to-all | bytes 196608 | tf_op jit(solution)/shard_map/all_to_all | solution.py:17
  191.2 0.1 reduce_sum.57
  191.3 0.0 reduce-scatter.2.cloned.1.call-done
  191.3 0.0 copy-start.2
  191.3 0.7 broadcast_in_dim.13
  192.0 3.9 %all-to-all-start.5 = ((bf16[32,2,768]{2,1,0:T(2,128)(2,1)}), bf16[32,2,768]{2,1,0:T(2,128)(2,1)S(1)}, u32[]{:S(2)}, u32[]{:S(2)}) async-start(bf16[32,2,768]{2,1,0:T(2,128)(2,1)} %broadcast_in_dim.13), calls=%async_computation.6 | async-start | bytes 196608 | tf_op jit(solution)/shard_map/all_to_all | solution.py:17
  195.9 0.0 copy-done.5
  195.9 0.2 fusion.6
  196.1 0.0 copy-done.6
  196.1 0.9 fusion
  197.1 0.0 copy-done.2
  197.1 1.1 slice_convert_fusion
  198.2 25.6 %all-to-all-done.5 = bf16[32,2,768]{2,1,0:T(2,128)(2,1)S(1)} async-done(((bf16[32,2,768]{2,1,0:T(2,128)(2,1)}), bf16[32,2,768]{2,1,0:T(2,128)(2,1)S(1)}, u32[]{:S(2)}, u32[]{:S(2)}) %all-to-all-start.5) | async-done | bytes 98336 | tf_op jit(solution)/shard_map/all_to_all | solution.py:17
  223.8 0.1 reduce_sum.58
  223.9 0.1 broadcast_in_dim.15
  223.9 12.3 %all_to_all.39 = bf16[32,2,768]{2,1,0:T(2,128)(2,1)S(1)} all-to-all(bf16[32,2,768]{2,1,0:T(2,128)(2,1)S(1)} %broadcast_in_dim.15), channel_id=1, replica_groups=mesh['x'=4,'y'=4,'z'=32,'c'=2] {'x','y','c'}, dimensions={0} | all-to-all | bytes 196608 | tf_op jit(solution)/shard_map/all_to_all | solution.py:17
  236.2 0.7 reshape.20
  (5 shorter events, 0.1 us)
Async XLA Ops:
  7.2 104.0 %all-gather.3.cloned.1.call-start = ((), (), s32[]{:S(2)}) async-start(), calls=%async_computation.9 | async-start | bytes 2949120 | tf_op jit(solution)/shard_map/all_gather | solution.py:188
  117.3 12.8 %all-to-all-start.2 = ((bf16[4,2,64,768]{3,2,1,0:T(8,128)(2,1)}), bf16[4,2,64,768]{3,2,1,0:T(8,128)(2,1)S(1)}, u32[]{:S(2)}, u32[]{:S(2)}) async-start(bf16[4,2,64,768]{3,2,1,0:T(8,128)(2,1)} %get-tuple-element.24), calls=%async_computation.2 | async-start | bytes 1572864 | tf_op jit(solution)/shard_map/all_to_all | solution.py:17
  120.8 70.5 %reduce-scatter.2.cloned.1.call-start = ((), (), s32[]{:S(2)}) async-start(), calls=%async_computation.8 | async-start | bytes 2949120 | tf_op jit(solution)/shard_map/reduce_scatter | solution.py:196
  125.5 50.9 %copy-start.1 = (bf16[1,196,768]{2,1,0:T(8,128)(2,1)S(1)}, bf16[1,196,768]{2,1,0:T(8,128)(2,1)}, u32[]{:S(2)}) copy-start(bf16[1,196,768]{2,1,0:T(8,128)(2,1)} %param.9) | copy-start | bytes 903172
  125.5 50.9 %copy-start.3 = (f32[196,64]{1,0:T(8,128)S(1)}, f32[196,64]{1,0:T(8,128)}, u32[]{:S(2)}) copy-start(f32[196,64]{1,0:T(8,128)} %get-tuple-element.21) | copy-start | bytes 150532
  130.2 46.6 %copy-start = (bf16[1,196,768]{2,1,0:T(8,128)(2,1)S(1)}, bf16[1,196,768]{2,1,0:T(8,128)(2,1)}, u32[]{:S(2)}) copy-start(bf16[1,196,768]{2,1,0:T(8,128)(2,1)} %param.5) | copy-start | bytes 903172
  130.2 46.6 %copy-start.4 = (f32[196,64]{1,0:T(8,128)S(1)}, f32[196,64]{1,0:T(8,128)}, u32[]{:S(2)}) copy-start(f32[196,64]{1,0:T(8,128)} %get-tuple-element.28) | copy-start | bytes 150532
  130.4 65.5 %copy-start.5 = (bf16[768,64]{0,1:T(8,128)(2,1)S(1)}, bf16[768,64]{0,1:T(8,128)(2,1)}, u32[]{:S(2)}) copy-start(bf16[768,64]{0,1:T(8,128)(2,1)} %param.6) | copy-start | bytes 294916
  130.6 65.5 %copy-start.6 = (bf16[196,64]{1,0:T(8,128)(2,1)S(1)}, bf16[196,64]{1,0:T(8,128)(2,1)}, u32[]{:S(2)}) copy-start(bf16[196,64]{1,0:T(8,128)(2,1)} %get-tuple-element.33) | copy-start | bytes 75268
  191.3 5.8 %copy-start.2 = (bf16[1,384,768]{2,1,0:T(8,128)(2,1)S(1)}, bf16[1,384,768]{2,1,0:T(8,128)(2,1)}, u32[]{:S(2)}) copy-start(bf16[1,384,768]{2,1,0:T(8,128)(2,1)} %reduce-scatter.2.cloned.1.call-done) | copy-start | bytes 1769476
  192.0 31.7 %all-to-all-start.5 = ((bf16[32,2,768]{2,1,0:T(2,128)(2,1)}), bf16[32,2,768]{2,1,0:T(2,128)(2,1)S(1)}, u32[]{:S(2)}, u32[]{:S(2)}) async-start(bf16[32,2,768]{2,1,0:T(2,128)(2,1)} %broadcast_in_dim.13), calls=%async_computation.6 | async-start | bytes 196608 | tf_op jit(solution)/shard_map/all_to_all | solution.py:17
Sparse Core Ops, SparseCore 0:
  28.2 59.2 all-gather.2
  130.3 34.6 reduce-scatter.1

commit v4 on v1

v4 whole, which is shorter than its diff:
```python
import jax
import jax.numpy as jnp
import numpy as np
from jax import lax
from jax.experimental import pallas as pl
from jax.experimental.pallas import tpu as pltpu
from jax.sharding import Mesh
from jax.sharding import PartitionSpec as P

BF = jnp.bfloat16
F32 = jnp.float32
ALL = ("x", "y", "z", "c")
VMEM_BYTES = 16 * 1024 * 1024


def exchange(parts, axes):
    return lax.all_to_all(parts, axes, split_axis=0, concat_axis=0, tiled=True)


def spread(mine, axes, count):
    return exchange(jnp.broadcast_to(mine[None], (count, *mine.shape)), axes)


def dot(a, b, dims):
    return lax.dot_general(a, b, (dims, ((), ())), preferred_element_type=F32)


def gelu_exact(value):
    return 0.5 * value * (1.0 + jax.scipy.special.erf(value * 0.7071067811865476))


def gelu_slope(value):
    return (
        0.5 * (1.0 + jax.scipy.special.erf(value * 0.7071067811865476))
        + value * jnp.exp(-0.5 * value * value) * 0.3989422804014327
    )


def weight_kernel(rows_in_ref, rows_grad_ref, act_ref, pre_ref, parts_ref):
    nx, double, _ = parts_ref.shape
    block = double // 2
    in_part = dot(pre_ref[...], rows_in_ref[...], ((0,), (0,))).astype(BF)
    out_part = dot(act_ref[...], rows_grad_ref[...], ((0,), (0,))).astype(BF)
    for i in range(nx):
        parts_ref[i, :block] = in_part[i * block : (i + 1) * block]
        parts_ref[i, block:] = out_part[i * block : (i + 1) * block]


def weight_parts(rows_in, rows_grad, act, pre_grad, nx):
    count, units = act.shape
    width = rows_in.shape[1]
    block = units // nx
    tile = min(256, width)
    columns = pl.BlockSpec((count, tile), lambda i: (0, i))
    whole = pl.BlockSpec((count, units), lambda i: (0, 0))
    return pl.pallas_call(
        weight_kernel,
        grid=(width // tile,),
        in_specs=[columns, columns, whole, whole],
        out_specs=pl.BlockSpec((nx, 2 * block, tile), lambda i: (0, 0, i)),
        out_shape=jax.ShapeDtypeStruct((nx, 2 * block, width), BF),
        compiler_params=pltpu.CompilerParams(vmem_limit_bytes=VMEM_BYTES),
        cost_estimate=pl.CostEstimate(
            flops=4 * count * units * width,
            bytes_accessed=4 * rows_in.size + 4 * act.size + 4 * units * width,
            transcendentals=0,
        ),
    )(rows_in, rows_grad, act, pre_grad)


def per_device(nx, ny, nz, nc, tokens, router, w_in, w_out, out_grad):
    tok, og = tokens[0], out_grad[0]
    width = tok.shape[1]
    experts = nz * nc
    block = w_out.shape[1]
    plane = nx * ny * nc

    weights = jnp.concatenate([w_in[0].T, w_out[0]], axis=0)
    gathered = lax.all_gather(weights, "x", axis=0, tiled=False)

    logits = jnp.dot(tok, router, preferred_element_type=F32)
    dispatch = jax.nn.softmax(logits, axis=0)
    combine = jax.nn.softmax(logits, axis=1)
    dispatch_b = dispatch.astype(BF)
    combine_b = combine.astype(BF)
    slots = dot(dispatch_b, tok, ((0,), (0,))).astype(BF)
    slot_grad = dot(combine_b, og, ((0,), (0,))).astype(BF)
    mine = exchange(jnp.stack([slots, slot_grad], axis=1), ("z", "c"))
    rows = spread(jnp.stack([mine[:, 0], mine[:, 1]], axis=0), "y", ny)
    first = gathered[:, :block].reshape(nx * block, width)
    second = gathered[:, block:].reshape(nx * block, width)
    rows, first, second = lax.optimization_barrier((rows, first, second))
    rows_in = rows[:, 0].reshape(ny * experts, width)
    rows_grad = rows[:, 1].reshape(ny * experts, width)

    hidden = dot(rows_in, first, ((1,), (1,)))
    act = gelu_exact(hidden).astype(BF)
    act_grad = dot(rows_grad, second, ((1,), (1,)))
    pre_grad = (act_grad * gelu_slope(hidden)).astype(BF)
    partial_out = dot(act, second, ((1,), (0,))).astype(BF)
    partial_in = dot(pre_grad, first, ((1,), (0,))).astype(BF)
    partial = jnp.stack(
        [partial_out.reshape(ny, experts, width), partial_in.reshape(ny, experts, width)], axis=1
    )
    parts_of_mine = exchange(partial, "y")
    parts = weight_parts(rows_in, rows_grad, act, pre_grad, nx)
    parts_of_mine, parts = lax.optimization_barrier((parts_of_mine, parts))
    grads = lax.psum_scatter(parts, "x", scatter_dimension=0, tiled=False)

    summed = parts_of_mine.astype(F32).sum(axis=0).astype(BF)
    back = exchange(jnp.stack([summed[0], summed[1]], axis=1), ("z", "c"))
    expert_out, slot_in_grad = back[:, 0], back[:, 1]

    combine_dot = dot(og, expert_out, ((1,), (1,)))
    combine_part = combine * (combine_dot - jnp.sum(combine * combine_dot, axis=1, keepdims=True))
    dispatch_dot = dot(tok, slot_in_grad, ((1,), (1,)))
    dispatch_part = dispatch * (
        dispatch_dot - jnp.sum(dispatch * dispatch_dot, axis=0, keepdims=True)
    )
    logit_grad = (combine_part + dispatch_part).astype(BF)

    local = dot(logit_grad, tok, ((0,), (0,))).astype(BF)
    pieces = exchange(local.reshape(plane, experts // plane, width), ("x", "y", "c"))
    piece = pieces.astype(F32).sum(axis=0).astype(BF)
    piece, grads, logit_grad = lax.optimization_barrier((piece, grads, logit_grad))
    along_z = spread(piece, "z", nz)
    w_in_grad = grads[:block].astype(F32)
    w_out_grad = grads[block:].astype(F32)
    token_grad = dot(logit_grad, router, ((1,), (1,))) + dot(
        dispatch_b, slot_in_grad, ((1,), (0,))
    )
    token_grad = token_grad.astype(BF)
    along_z, w_in_grad, w_out_grad, token_grad = lax.optimization_barrier(
        (along_z, w_in_grad, w_out_grad, token_grad)
    )
    total = along_z.astype(F32).sum(axis=0).astype(BF)
    router_grad = spread(total, ("x", "y", "c"), plane).reshape(experts, width).astype(F32).T
    return token_grad[None], router_grad, w_in_grad.T[None], w_out_grad[None]


def solution(mesh):
    dp, expert = mesh.shape["dp"], mesh.shape["expert"]
    nx, ny, nz, nc = 4, dp // 4, expert // 2, 2
    fine = Mesh(np.asarray(mesh.devices).reshape(nx, ny, nz, nc), ALL)

    def run(*args):
        return per_device(nx, ny, nz, nc, *args)

    return jax.shard_map(
        run,
        mesh=fine,
        in_specs=(
            P(ALL, None, None),
            P(),
            P(("z", "c"), None, ("x", "y")),
            P(("z", "c"), ("x", "y"), None),
            P(ALL, None, None),
        ),
        out_specs=(
            P(ALL, None, None),
            P(),
            P(("z", "c"), None, ("x", "y")),
            P(("z", "c"), ("x", "y"), None),
        ),
        check_vma=False,
    )
```

time: 229 us -> 224 us (0.978)
  blocking collectives: 152 us -> 139 us
  waiting for transfers between devices: 34.1 us -> 39 us
  Pallas kernels: 0 us -> 2.88 us
  starting transfers between devices: 9.27 us -> 11.6 us
    all_to_all x5 -> x4, blocking collectives: 152 us -> 139 us  [exchange(): return lax.all_to_all(parts, axes, split_axis=0, concat_axis=0, tiled=True)]
    all_to_all x2 -> x3, waiting for transfers between devices: 34.1 us -> 39 us  [exchange(): return lax.all_to_all(parts, axes, split_axis=0, concat_axis=0, tiled=True)]
    pallas_call x0 -> x1, Pallas kernels: none -> 2.88 us  [weight_parts(): pl.pallas_call(weight_kernel, grid=(width // tile,), in_specs=[columns, c...]
    all_to_all x2 -> x3, starting transfers between devices: 9.19 us -> 11.5 us  [exchange(): return lax.all_to_all(parts, axes, split_axis=0, concat_axis=0, tiled=True)]
    dot_general x13 -> x11, matrix products: 5.76 us -> 4.47 us  [dot(): return lax.dot_general(a, b, (dims, ((), ())), preferred_element_type=F32)]
  transfers between devices with their start and end apart: 4 -> 5, of which waited for: 2 -> 3; matrix products, arithmetic and copies ran while one was open for 3% -> 4% of each run, Pallas kernels for 0% -> 1%
where the time goes in v4:
time: 224 us; the launch traced here: 223 us
  blocking collectives  139 us (62%)
  waiting for transfers between devices  39 us (17%)
  between operations  14.3 us (6%)
  starting transfers between devices  11.6 us (5%)
  local copies, waits for them, and re-layouts  7.04 us (3%)
  matrix products  4.81 us (2%)
  other arithmetic  4.71 us (2%)
  Pallas kernels  2.88 us (1%)
    all_to_all x4, blocking collectives, exchange(): return lax.all_to_all(parts, axes, split_axis=0, concat_axis=0, tiled=True)  139 us
    all_to_all x3, waiting for transfers between devices, exchange(): return lax.all_to_all(parts, axes, split_axis=0, concat_axis=0, tiled=True)  39 us
    all_to_all x3, starting transfers between devices, exchange(): return lax.all_to_all(parts, axes, split_axis=0, concat_axis=0, tiled=True)  11.5 us
  transfers between devices with their start and end apart: 5, of which 3 were waited for; matrix products, arithmetic and copies ran while one was open for 4% of the time, Pallas kernels for 1%

profile of v4, /device:TPU:1, one launch (start us, length us, event | category | flops | bytes accessed | tf_op | source)
XLA Modules:
  0.0 223.3 jit_solution(7386187501765821021)
XLA Ops:
  7.2 0.0 copy-start
  7.2 0.0 copy-start.3
  7.2 0.0 copy-start.4
  7.2 0.0 all-gather.3.cloned.1.call-start
  7.2 2.0 pad_maximum_fusion.1
  9.2 0.0 all-gather.3.cloned.1.call-update
  9.2 0.0 copy-done
  9.2 0.0 copy-done.3
  9.3 0.3 fusion.25
  9.6 0.2 fusion.18
  9.8 0.0 copy-done.4
  9.8 0.2 fusion.3
  10.0 0.2 fusion.2
  10.3 0.2 copy.14
  10.5 66.8 %all_to_all.35 = bf16[64,2,768]{2,1,0:T(2,128)(2,1)S(1)} all-to-all(bf16[64,2,768]{2,1,0:T(2,128)(2,1)S(1)} %copy.14), channel_id=1, replica_groups=mesh['x'=4,'y'=4,'z'=32,'c'=2] {'z','c'}, dimensions={0} | all-to-all | bytes 393216 | tf_op jit(solution)/shard_map/all_to_all | solution.py:17
  77.3 0.3 fusion.29
  77.7 0.9 broadcast_in_dim.12
  78.6 4.2 %all-to-all-start.1 = ((bf16[4,2,64,768]{3,2,1,0:T(8,128)(2,1)}), bf16[4,2,64,768]{3,2,1,0:T(8,128)(2,1)S(1)}, u32[]{:S(2)}, u32[]{:S(2)}) async-start(bf16[4,2,64,768]{3,2,1,0:T(8,128)(2,1)} %broadcast_in_dim.12), calls=%async_computation.1 | async-start | bytes 1572864 | tf_op jit(solution)/shard_map/all_to_all | solution.py:17
  82.8 0.0 all-gather.3.cloned.1.call-done
  82.8 2.8 %fusion.26 = (bf16[4,192,768]{2,1,0:T(8,128)(2,1)}, bf16[4,192,768]{2,1,0:T(8,128)(2,1)S(1)}) fusion(bf16[4,384,768]{2,1,0:T(8,128)(2,1)} %bitcast.85), kind=kLoop, calls=%fused_computation.53 | loop fusion | bytes 4718592 | tf_op jit(solution)/shard_map/slice | solution.py:91
  85.6 7.5 %all-to-all-done.1 = bf16[4,2,64,768]{3,2,1,0:T(8,128)(2,1)S(1)} async-done(((bf16[4,2,64,768]{3,2,1,0:T(8,128)(2,1)}), bf16[4,2,64,768]{3,2,1,0:T(8,128)(2,1)S(1)}, u32[]{:S(2)}, u32[]{:S(2)}) %all-to-all-start.1) | async-done | bytes 786464 | tf_op jit(solution)/shard_map/all_to_all | solution.py:17
  93.0 0.1 fusion.27
  93.1 0.0 copy-start.1
  93.1 0.5 multiply_convert_fusion
  93.6 0.7 copy-done.1
  94.4 0.5 convolution_convert_fusion.1
  94.9 0.6 fusion.pre_ref
  95.4 0.5 convolution_convert_fusion
  95.9 1.0 pad_maximum_fusion
  96.9 3.5 %all-to-all-start.2 = ((bf16[4,2,64,768]{3,2,1,0:T(8,128)(2,1)}), bf16[4,2,64,768]{3,2,1,0:T(8,128)(2,1)S(1)}, u32[]{:S(2)}, u32[]{:S(2)}) async-start(bf16[4,2,64,768]{3,2,1,0:T(8,128)(2,1)} %pad_maximum_fusion), calls=%async_computation.2 | async-start | bytes 1572864 | tf_op jit(solution)/shard_map/all_to_all | solution.py:17
  100.4 0.0 reduce-scatter.2.cloned.1.call-start
  100.4 2.9 %shard_map.84 = bf16[4,384,768]{2,1,0:T(8,128)(2,1)} custom-call(bf16[256,768]{1,0:T(8,128)(2,1)S(1)} %bitcast.78, bf16[256,768]{1,0:T(8,128)(2,1)S(1)} %bitcast.80, bf16[256,768]{1,0:T(8,128)(2,1)S(1)} %get-tuple-element.47.act_ref, bf16[256,768]{1,0:T(8,128)(2,1)S(1)} %fusion.pre_ref), custom_call_target="tpu_custom_call" | custom-call | flops 603979776 | bytes 3932160 | tf_op jit(solution)/shard_map/pallas_call | solution.py:56
  103.3 6.1 %all-to-all-done.2 = bf16[4,2,64,768]{3,2,1,0:T(8,128)(2,1)S(1)} async-done(((bf16[4,2,64,768]{3,2,1,0:T(8,128)(2,1)}), bf16[4,2,64,768]{3,2,1,0:T(8,128)(2,1)S(1)}, u32[]{:S(2)}, u32[]{:S(2)}) %all-to-all-start.2) | async-done | bytes 786464 | tf_op jit(solution)/shard_map/all_to_all | solution.py:17
  109.4 0.0 reduce-scatter.2.cloned.1.call-update
  109.4 0.1 reduce_sum.74
  109.6 0.2 copy.19
  109.8 46.0 %all_to_all.36 = bf16[64,2,768]{2,1,0:T(2,128)(2,1)S(1)} all-to-all(bf16[64,2,768]{2,1,0:T(2,128)(2,1)S(1)} %copy.19), channel_id=1, replica_groups=mesh['x'=4,'y'=4,'z'=32,'c'=2] {'z','c'}, dimensions={0} | all-to-all | bytes 393216 | tf_op jit(solution)/shard_map/all_to_all | solution.py:17
  155.8 0.3 fusion.28
  156.1 0.2 convolution_bitcast_fusion
  156.3 0.3 multiply_reduce_fusion.1
  156.6 0.1 add_convert_fusion
  156.7 0.2 convolution_convert_fusion.2
  156.9 13.8 %all_to_all.37 = bf16[32,2,768]{2,1,0:T(2,128)(2,1)S(1)} all-to-all(bf16[32,2,768]{2,1,0:T(2,128)(2,1)S(1)} %reshape.31), channel_id=1, replica_groups=mesh['x'=4,'y'=4,'z'=32,'c'=2] {'x','y','c'}, dimensions={0} | all-to-all | bytes 196608 | tf_op jit(solution)/shard_map/all_to_all | solution.py:17
  170.7 0.1 reduce_sum.77
  170.8 0.0 reduce-scatter.2.cloned.1.call-done
  170.9 0.0 copy-start.2
  170.9 0.7 broadcast_in_dim.13
  171.6 3.9 %all-to-all-start.5 = ((bf16[32,2,768]{2,1,0:T(2,128)(2,1)}), bf16[32,2,768]{2,1,0:T(2,128)(2,1)S(1)}, u32[]{:S(2)}, u32[]{:S(2)}) async-start(bf16[32,2,768]{2,1,0:T(2,128)(2,1)} %broadcast_in_dim.13), calls=%async_computation.6 | async-start | bytes 196608 | tf_op jit(solution)/shard_map/all_to_all | solution.py:17
  175.4 0.3 fusion.30
  175.7 1.1 fusion.1
  176.8 0.0 copy-done.2
  176.8 1.1 slice_convert_fusion
  177.8 25.4 %all-to-all-done.5 = bf16[32,2,768]{2,1,0:T(2,128)(2,1)S(1)} async-done(((bf16[32,2,768]{2,1,0:T(2,128)(2,1)}), bf16[32,2,768]{2,1,0:T(2,128)(2,1)S(1)}, u32[]{:S(2)}, u32[]{:S(2)}) %all-to-all-start.5) | async-done | bytes 98336 | tf_op jit(solution)/shard_map/all_to_all | solution.py:17
  203.3 0.1 reduce_sum.78
  203.4 0.1 broadcast_in_dim.15
  203.4 12.3 %all_to_all.38 = bf16[32,2,768]{2,1,0:T(2,128)(2,1)S(1)} all-to-all(bf16[32,2,768]{2,1,0:T(2,128)(2,1)S(1)} %broadcast_in_dim.15), channel_id=1, replica_groups=mesh['x'=4,'y'=4,'z'=32,'c'=2] {'x','y','c'}, dimensions={0} | all-to-all | bytes 196608 | tf_op jit(solution)/shard_map/all_to_all | solution.py:17
  215.7 0.7 reshape.32
  (6 shorter events, 0.2 us)
Async XLA Ops:
  7.2 2.1 copy-start
  7.2 2.1 copy-start.3
  7.2 2.6 %copy-start.4 = (bf16[1,196,768]{2,1,0:T(8,128)(2,1)S(1)}, bf16[1,196,768]{2,1,0:T(8,128)(2,1)}, u32[]{:S(2)}) copy-start(bf16[1,196,768]{2,1,0:T(8,128)(2,1)} %param.9) | copy-start | bytes 903172
  7.2 75.6 %all-gather.3.cloned.1.call-start = ((), (), s32[]{:S(2)}) async-start(), calls=%async_computation.9 | async-start | bytes 2949120 | tf_op jit(solution)/shard_map/all_gather | solution.py:79
  78.6 14.4 %all-to-all-start.1 = ((bf16[4,2,64,768]{3,2,1,0:T(8,128)(2,1)}), bf16[4,2,64,768]{3,2,1,0:T(8,128)(2,1)S(1)}, u32[]{:S(2)}, u32[]{:S(2)}) async-start(bf16[4,2,64,768]{3,2,1,0:T(8,128)(2,1)} %broadcast_in_dim.12), calls=%async_computation.1 | async-start | bytes 1572864 | tf_op jit(solution)/shard_map/all_to_all | solution.py:17
  93.1 1.3 copy-start.1
  96.9 12.5 %all-to-all-start.2 = ((bf16[4,2,64,768]{3,2,1,0:T(8,128)(2,1)}), bf16[4,2,64,768]{3,2,1,0:T(8,128)(2,1)S(1)}, u32[]{:S(2)}, u32[]{:S(2)}) async-start(bf16[4,2,64,768]{3,2,1,0:T(8,128)(2,1)} %pad_maximum_fusion), calls=%async_computation.2 | async-start | bytes 1572864 | tf_op jit(solution)/shard_map/all_to_all | solution.py:17
  100.4 70.5 %reduce-scatter.2.cloned.1.call-start = ((), (), s32[]{:S(2)}) async-start(), calls=%async_computation.8 | async-start | bytes 2949120 | tf_op jit(solution)/shard_map/reduce_scatter | solution.py:108
  170.9 5.9 %copy-start.2 = (bf16[1,384,768]{2,1,0:T(8,128)(2,1)S(1)}, bf16[1,384,768]{2,1,0:T(8,128)(2,1)}, u32[]{:S(2)}) copy-start(bf16[1,384,768]{2,1,0:T(8,128)(2,1)} %reduce-scatter.2.cloned.1.call-done) | copy-start | bytes 1769476
  171.6 31.7 %all-to-all-start.5 = ((bf16[32,2,768]{2,1,0:T(2,128)(2,1)}), bf16[32,2,768]{2,1,0:T(2,128)(2,1)S(1)}, u32[]{:S(2)}, u32[]{:S(2)}) async-start(bf16[32,2,768]{2,1,0:T(2,128)(2,1)} %broadcast_in_dim.13), calls=%async_computation.6 | async-start | bytes 196608 | tf_op jit(solution)/shard_map/all_to_all | solution.py:17
Sparse Core Ops, SparseCore 0:
  11.3 59.2 all-gather.2
  109.5 35.2 reduce-scatter.1

commit v5 on v4

--- a/solution.py
+++ b/solution.py
@@ -85,8 +85,10 @@
     combine_b = combine.astype(BF)
     slots = dot(dispatch_b, tok, ((0,), (0,))).astype(BF)
     slot_grad = dot(combine_b, og, ((0,), (0,))).astype(BF)
-    mine = exchange(jnp.stack([slots, slot_grad], axis=1), ("z", "c"))
-    rows = spread(jnp.stack([mine[:, 0], mine[:, 1]], axis=0), "y", ny)
+    sent = jnp.stack([slots, slot_grad], axis=1).reshape(nz, nc * 2, width)
+    mine = exchange(sent, "z").reshape(nz, nc, 2, width).transpose(1, 2, 0, 3)
+    copies = jnp.broadcast_to(mine[None], (ny, nc, 2, nz, width))
+    rows = exchange(copies.reshape(ny * nc, 2, nz, width), ("y", "c"))
     first = gathered[:, :block].reshape(nx * block, width)
     second = gathered[:, block:].reshape(nx * block, width)
     rows, first, second = lax.optimization_barrier((rows, first, second))
@@ -99,16 +101,16 @@
     pre_grad = (act_grad * gelu_slope(hidden)).astype(BF)
     partial_out = dot(act, second, ((1,), (0,))).astype(BF)
     partial_in = dot(pre_grad, first, ((1,), (0,))).astype(BF)
-    partial = jnp.stack(
-        [partial_out.reshape(ny, experts, width), partial_in.reshape(ny, experts, width)], axis=1
-    )
-    parts_of_mine = exchange(partial, "y")
+    shape = (ny * nc, nz, width)
+    partial = jnp.stack([partial_out.reshape(shape), partial_in.reshape(shape)], axis=1)
+    parts_of_mine = exchange(partial, ("y", "c"))
     parts = weight_parts(rows_in, rows_grad, act, pre_grad, nx)
     parts_of_mine, parts = lax.optimization_barrier((parts_of_mine, parts))
     grads = lax.psum_scatter(parts, "x", scatter_dimension=0, tiled=False)
 
-    summed = parts_of_mine.astype(F32).sum(axis=0).astype(BF)
-    back = exchange(jnp.stack([summed[0], summed[1]], axis=1), ("z", "c"))
+    summed = parts_of_mine.reshape(ny, nc, 2, nz, width).astype(F32).sum(axis=0).astype(BF)
+    back = exchange(summed.transpose(2, 0, 1, 3).reshape(nz, nc * 2, width), "z")
+    back = back.reshape(experts, 2, width)
     expert_out, slot_in_grad = back[:, 0], back[:, 1]
 
     combine_dot = dot(og, expert_out, ((1,), (1,)))

time: 224 us -> 224 us (level)
  blocking collectives: 139 us -> 130 us
  waiting for transfers between devices: 39 us -> 44.4 us
  starting transfers between devices: 11.6 us -> 15.1 us
    all_to_all x4, blocking collectives: 139 us -> 130 us  [exchange(): return lax.all_to_all(parts, axes, split_axis=0, concat_axis=0, tiled=True)]
    all_to_all x3, waiting for transfers between devices: 39 us -> 44.4 us  [exchange(): return lax.all_to_all(parts, axes, split_axis=0, concat_axis=0, tiled=True)]
    all_to_all x3, starting transfers between devices: 11.5 us -> 15.1 us  [exchange(): return lax.all_to_all(parts, axes, split_axis=0, concat_axis=0, tiled=True)]
where the time goes in v5:
time: 224 us; the launch traced here: 223 us
  blocking collectives  130 us (58%)
  waiting for transfers between devices  44.4 us (20%)
  starting transfers between devices  15.1 us (7%)
  between operations  14.2 us (6%)
  local copies, waits for them, and re-layouts  6.88 us (3%)
  matrix products  4.81 us (2%)
  other arithmetic  4.67 us (2%)
  Pallas kernels  2.86 us (1%)
    all_to_all x4, blocking collectives, exchange(): return lax.all_to_all(parts, axes, split_axis=0, concat_axis=0, tiled=True)  130 us
    all_to_all x3, waiting for transfers between devices, exchange(): return lax.all_to_all(parts, axes, split_axis=0, concat_axis=0, tiled=True)  44.4 us
    all_to_all x3, starting transfers between devices, exchange(): return lax.all_to_all(parts, axes, split_axis=0, concat_axis=0, tiled=True)  15.1 us
  transfers between devices with their start and end apart: 5, of which 3 were waited for; matrix products, arithmetic and copies ran while one was open for 4% of the time, Pallas kernels for 1%

profile of v5, /device:TPU:1, one launch (start us, length us, event | category | flops | bytes accessed | tf_op | source)
XLA Modules:
  0.0 223.1 jit_solution(17249409292339712498)
XLA Ops:
  7.2 0.0 copy-start
  7.2 0.0 copy-start.3
  7.2 0.0 copy-start.4
  7.2 0.0 all-gather.3.cloned.1.call-start
  7.2 2.0 pad_maximum_fusion.1
  9.2 0.0 all-gather.3.cloned.1.call-update
  9.2 0.0 copy-done
  9.2 0.0 copy-done.3
  9.3 0.3 fusion.31
  9.6 0.2 fusion.22
  9.8 0.0 copy-done.4
  9.8 0.2 fusion.3
  10.0 0.2 fusion.2
  10.3 0.2 copy.24
  10.5 0.1 reshape.47
  10.6 64.5 %all_to_all.35 = bf16[32,4,768]{2,1,0:T(4,128)(2,1)S(1)} all-to-all(bf16[32,4,768]{2,1,0:T(4,128)(2,1)S(1)} %reshape.47), channel_id=1, replica_groups=mesh['x'=4,'y'=4,'z'=32,'c'=2] {'z'}, dimensions={0} | all-to-all | bytes 393216 | tf_op jit(solution)/shard_map/all_to_all | solution.py:17
  75.1 1.0 broadcast_in_dim.12
  76.1 6.9 %all-to-all-start.1 = ((bf16[8,2,32,768]{3,2,1,0:T(8,128)(2,1)}), bf16[8,2,32,768]{3,2,1,0:T(8,128)(2,1)S(1)}, u32[]{:S(2)}, u32[]{:S(2)}) async-start(bf16[8,2,32,768]{3,2,1,0:T(8,128)(2,1)} %bitcast.6), calls=%async_computation.1 | async-start | bytes 1572864 | tf_op jit(solution)/shard_map/all_to_all | solution.py:17
  82.9 0.0 all-gather.3.cloned.1.call-done
  82.9 2.8 %fusion.32 = (bf16[4,192,768]{2,1,0:T(8,128)(2,1)}, bf16[4,192,768]{2,1,0:T(8,128)(2,1)S(1)}) fusion(bf16[4,384,768]{2,1,0:T(8,128)(2,1)} %bitcast.89), kind=kLoop, calls=%fused_computation.51 | loop fusion | bytes 4718592 | tf_op jit(solution)/shard_map/slice | solution.py:93
  85.7 9.5 %all-to-all-done.1 = bf16[8,2,32,768]{3,2,1,0:T(8,128)(2,1)S(1)} async-done(((bf16[8,2,32,768]{3,2,1,0:T(8,128)(2,1)}), bf16[8,2,32,768]{3,2,1,0:T(8,128)(2,1)S(1)}, u32[]{:S(2)}, u32[]{:S(2)}) %all-to-all-start.1) | async-done | bytes 786464 | tf_op jit(solution)/shard_map/all_to_all | solution.py:17
  95.2 0.1 fusion.33
  95.3 0.0 copy-start.1
  95.3 0.5 multiply_convert_fusion
  95.8 0.7 copy-done.1
  96.6 0.5 convolution_convert_fusion.1
  97.0 0.6 fusion.pre_ref
  97.6 0.5 convolution_convert_fusion
  98.1 1.0 pad_maximum_fusion
  99.1 4.3 %all-to-all-start.2 = ((bf16[8,2,32,768]{3,2,1,0:T(8,128)(2,1)}), bf16[8,2,32,768]{3,2,1,0:T(8,128)(2,1)S(1)}, u32[]{:S(2)}, u32[]{:S(2)}) async-start(bf16[8,2,32,768]{3,2,1,0:T(8,128)(2,1)} %pad_maximum_fusion), calls=%async_computation.2 | async-start | bytes 1572864 | tf_op jit(solution)/shard_map/all_to_all | solution.py:17
  103.4 0.0 reduce-scatter.2.cloned.1.call-start
  103.4 2.9 %shard_map.84 = bf16[4,384,768]{2,1,0:T(8,128)(2,1)} custom-call(bf16[256,768]{1,0:T(8,128)(2,1)S(1)} %bitcast.81, bf16[256,768]{1,0:T(8,128)(2,1)S(1)} %bitcast.83, bf16[256,768]{1,0:T(8,128)(2,1)S(1)} %get-tuple-element.43.act_ref, bf16[256,768]{1,0:T(8,128)(2,1)S(1)} %fusion.pre_ref), custom_call_target="tpu_custom_call" | custom-call | flops 603979776 | bytes 3932160 | tf_op jit(solution)/shard_map/pallas_call | solution.py:56
  106.3 9.4 %all-to-all-done.2 = bf16[8,2,32,768]{3,2,1,0:T(8,128)(2,1)S(1)} async-done(((bf16[8,2,32,768]{3,2,1,0:T(8,128)(2,1)}), bf16[8,2,32,768]{3,2,1,0:T(8,128)(2,1)S(1)}, u32[]{:S(2)}, u32[]{:S(2)}) %all-to-all-start.2) | async-done | bytes 786464 | tf_op jit(solution)/shard_map/all_to_all | solution.py:17
  115.7 0.0 reduce-scatter.2.cloned.1.call-update
  115.7 0.1 reduce_sum.74
  115.9 0.2 copy.30
  116.0 38.4 %all_to_all.36 = bf16[32,4,768]{2,1,0:T(4,128)(2,1)S(1)} all-to-all(bf16[32,4,768]{2,1,0:T(4,128)(2,1)S(1)} %copy.30), channel_id=1, replica_groups=mesh['x'=4,'y'=4,'z'=32,'c'=2] {'z'}, dimensions={0} | all-to-all | bytes 393216 | tf_op jit(solution)/shard_map/all_to_all | solution.py:17
  154.4 0.1 reshape.54
  154.5 0.3 fusion.34
  154.8 0.2 convolution_bitcast_fusion
  155.0 0.3 multiply_reduce_fusion.1
  155.3 0.1 add_convert_fusion
  155.4 0.2 convolution_convert_fusion.2
  155.6 14.9 %all_to_all.37 = bf16[32,2,768]{2,1,0:T(2,128)(2,1)S(1)} all-to-all(bf16[32,2,768]{2,1,0:T(2,128)(2,1)S(1)} %reshape.55), channel_id=1, replica_groups=mesh['x'=4,'y'=4,'z'=32,'c'=2] {'x','y','c'}, dimensions={0} | all-to-all | bytes 196608 | tf_op jit(solution)/shard_map/all_to_all | solution.py:17
  170.6 0.1 reduce_sum.77
  170.7 0.0 reduce-scatter.2.cloned.1.call-done
  170.7 0.0 copy-start.2
  170.7 0.7 broadcast_in_dim.13
  171.4 3.9 %all-to-all-start.5 = ((bf16[32,2,768]{2,1,0:T(2,128)(2,1)}), bf16[32,2,768]{2,1,0:T(2,128)(2,1)S(1)}, u32[]{:S(2)}, u32[]{:S(2)}) async-start(bf16[32,2,768]{2,1,0:T(2,128)(2,1)} %broadcast_in_dim.13), calls=%async_computation.6 | async-start | bytes 196608 | tf_op jit(solution)/shard_map/all_to_all | solution.py:17
  175.3 0.3 fusion.35
  175.5 1.1 fusion.1
  176.6 0.0 copy-done.2
  176.6 1.1 slice_convert_fusion
  177.7 25.4 %all-to-all-done.5 = bf16[32,2,768]{2,1,0:T(2,128)(2,1)S(1)} async-done(((bf16[32,2,768]{2,1,0:T(2,128)(2,1)}), bf16[32,2,768]{2,1,0:T(2,128)(2,1)S(1)}, u32[]{:S(2)}, u32[]{:S(2)}) %all-to-all-start.5) | async-done | bytes 98336 | tf_op jit(solution)/shard_map/all_to_all | solution.py:17
  203.1 0.1 reduce_sum.78
  203.2 0.1 broadcast_in_dim.15
  203.3 12.3 %all_to_all.38 = bf16[32,2,768]{2,1,0:T(2,128)(2,1)S(1)} all-to-all(bf16[32,2,768]{2,1,0:T(2,128)(2,1)S(1)} %broadcast_in_dim.15), channel_id=1, replica_groups=mesh['x'=4,'y'=4,'z'=32,'c'=2] {'x','y','c'}, dimensions={0} | all-to-all | bytes 196608 | tf_op jit(solution)/shard_map/all_to_all | solution.py:17
  215.6 0.7 reshape.56
  (3 shorter events, 0.1 us)
Async XLA Ops:
  7.2 2.1 copy-start
  7.2 2.1 copy-start.3
  7.2 2.6 %copy-start.4 = (bf16[1,196,768]{2,1,0:T(8,128)(2,1)S(1)}, bf16[1,196,768]{2,1,0:T(8,128)(2,1)}, u32[]{:S(2)}) copy-start(bf16[1,196,768]{2,1,0:T(8,128)(2,1)} %param.9) | copy-start | bytes 903172
  7.2 75.7 %all-gather.3.cloned.1.call-start = ((), (), s32[]{:S(2)}) async-start(), calls=%async_computation.9 | async-start | bytes 2949120 | tf_op jit(solution)/shard_map/all_gather | solution.py:79
  76.1 19.2 %all-to-all-start.1 = ((bf16[8,2,32,768]{3,2,1,0:T(8,128)(2,1)}), bf16[8,2,32,768]{3,2,1,0:T(8,128)(2,1)S(1)}, u32[]{:S(2)}, u32[]{:S(2)}) async-start(bf16[8,2,32,768]{3,2,1,0:T(8,128)(2,1)} %bitcast.6), calls=%async_computation.1 | async-start | bytes 1572864 | tf_op jit(solution)/shard_map/all_to_all | solution.py:17
  95.3 1.3 copy-start.1
  99.1 16.6 %all-to-all-start.2 = ((bf16[8,2,32,768]{3,2,1,0:T(8,128)(2,1)}), bf16[8,2,32,768]{3,2,1,0:T(8,128)(2,1)S(1)}, u32[]{:S(2)}, u32[]{:S(2)}) async-start(bf16[8,2,32,768]{3,2,1,0:T(8,128)(2,1)} %pad_maximum_fusion), calls=%async_computation.2 | async-start | bytes 1572864 | tf_op jit(solution)/shard_map/all_to_all | solution.py:17
  103.4 67.3 %reduce-scatter.2.cloned.1.call-start = ((), (), s32[]{:S(2)}) async-start(), calls=%async_computation.8 | async-start | bytes 2949120 | tf_op jit(solution)/shard_map/reduce_scatter | solution.py:109
  170.7 5.9 %copy-start.2 = (bf16[1,384,768]{2,1,0:T(8,128)(2,1)S(1)}, bf16[1,384,768]{2,1,0:T(8,128)(2,1)}, u32[]{:S(2)}) copy-start(bf16[1,384,768]{2,1,0:T(8,128)(2,1)} %reduce-scatter.2.cloned.1.call-done) | copy-start | bytes 1769476
  171.4 31.7 %all-to-all-start.5 = ((bf16[32,2,768]{2,1,0:T(2,128)(2,1)}), bf16[32,2,768]{2,1,0:T(2,128)(2,1)S(1)}, u32[]{:S(2)}, u32[]{:S(2)}) async-start(bf16[32,2,768]{2,1,0:T(2,128)(2,1)} %broadcast_in_dim.13), calls=%async_computation.6 | async-start | bytes 196608 | tf_op jit(solution)/shard_map/all_to_all | solution.py:17
Sparse Core Ops, SparseCore 0:
  11.3 59.2 all-gather.2
  115.9 29.2 reduce-scatter.1

commit v6 on v5

--- a/solution.py
+++ b/solution.py
@@ -9,7 +9,10 @@
 
 BF = jnp.bfloat16
 F32 = jnp.float32
-ALL = ("x", "y", "z", "c")
+Z = ("zh", "zl")
+ALL = ("x", "y", "zh", "zl", "c")
+EXPERT = ("zh", "zl", "c")
+BOX = ("x", "y", "zl", "c")
 VMEM_BYTES = 16 * 1024 * 1024
 
 
@@ -68,12 +71,12 @@
     )(rows_in, rows_grad, act, pre_grad)
 
 
-def per_device(nx, ny, nz, nc, tokens, router, w_in, w_out, out_grad):
+def per_device(nx, ny, nz, nl, nc, tokens, router, w_in, w_out, out_grad):
     tok, og = tokens[0], out_grad[0]
     width = tok.shape[1]
     experts = nz * nc
     block = w_out.shape[1]
-    plane = nx * ny * nc
+    box = nx * ny * nl * nc
 
     weights = jnp.concatenate([w_in[0].T, w_out[0]], axis=0)
     gathered = lax.all_gather(weights, "x", axis=0, tiled=False)
@@ -86,7 +89,7 @@
     slots = dot(dispatch_b, tok, ((0,), (0,))).astype(BF)
     slot_grad = dot(combine_b, og, ((0,), (0,))).astype(BF)
     sent = jnp.stack([slots, slot_grad], axis=1).reshape(nz, nc * 2, width)
-    mine = exchange(sent, "z").reshape(nz, nc, 2, width).transpose(1, 2, 0, 3)
+    mine = exchange(sent, Z).reshape(nz, nc, 2, width).transpose(1, 2, 0, 3)
     copies = jnp.broadcast_to(mine[None], (ny, nc, 2, nz, width))
     rows = exchange(copies.reshape(ny * nc, 2, nz, width), ("y", "c"))
     first = gathered[:, :block].reshape(nx * block, width)
@@ -109,7 +112,7 @@
     grads = lax.psum_scatter(parts, "x", scatter_dimension=0, tiled=False)
 
     summed = parts_of_mine.reshape(ny, nc, 2, nz, width).astype(F32).sum(axis=0).astype(BF)
-    back = exchange(summed.transpose(2, 0, 1, 3).reshape(nz, nc * 2, width), "z")
+    back = exchange(summed.transpose(2, 0, 1, 3).reshape(nz, nc * 2, width), Z)
     back = back.reshape(experts, 2, width)
     expert_out, slot_in_grad = back[:, 0], back[:, 1]
 
@@ -122,10 +125,10 @@
     logit_grad = (combine_part + dispatch_part).astype(BF)
 
     local = dot(logit_grad, tok, ((0,), (0,))).astype(BF)
-    pieces = exchange(local.reshape(plane, experts // plane, width), ("x", "y", "c"))
+    pieces = exchange(local.reshape(box, 2, -1), BOX)
     piece = pieces.astype(F32).sum(axis=0).astype(BF)
     piece, grads, logit_grad = lax.optimization_barrier((piece, grads, logit_grad))
-    along_z = spread(piece, "z", nz)
+    along_z = spread(piece, "zh", nz // nl)
     w_in_grad = grads[:block].astype(F32)
     w_out_grad = grads[block:].astype(F32)
     token_grad = dot(logit_grad, router, ((1,), (1,))) + dot(
@@ -136,17 +139,17 @@
         (along_z, w_in_grad, w_out_grad, token_grad)
     )
     total = along_z.astype(F32).sum(axis=0).astype(BF)
-    router_grad = spread(total, ("x", "y", "c"), plane).reshape(experts, width).astype(F32).T
+    router_grad = spread(total, BOX, box).reshape(experts, width).astype(F32).T
     return token_grad[None], router_grad, w_in_grad.T[None], w_out_grad[None]
 
 
 def solution(mesh):
     dp, expert = mesh.shape["dp"], mesh.shape["expert"]
-    nx, ny, nz, nc = 4, dp // 4, expert // 2, 2
-    fine = Mesh(np.asarray(mesh.devices).reshape(nx, ny, nz, nc), ALL)
+    nx, ny, nz, nl, nc = 4, dp // 4, expert // 2, 2, 2
+    fine = Mesh(np.asarray(mesh.devices).reshape(nx, ny, nz // nl, nl, nc), ALL)
 
     def run(*args):
-        return per_device(nx, ny, nz, nc, *args)
+        return per_device(nx, ny, nz, nl, nc, *args)
 
     return jax.shard_map(
         run,
@@ -154,15 +157,15 @@
         in_specs=(
             P(ALL, None, None),
             P(),
-            P(("z", "c"), None, ("x", "y")),
-            P(("z", "c"), ("x", "y"), None),
+            P(EXPERT, None, ("x", "y")),
+            P(EXPERT, ("x", "y"), None),
             P(ALL, None, None),
         ),
         out_specs=(
             P(ALL, None, None),
             P(),
-            P(("z", "c"), None, ("x", "y")),
-            P(("z", "c"), ("x", "y"), None),
+            P(EXPERT, None, ("x", "y")),
+            P(EXPERT, ("x", "y"), None),
         ),
         check_vma=False,
     )

time: 224 us -> 219 us (0.978)
  waiting for transfers between devices: 44.4 us -> 37.5 us
  blocking collectives: 130 us -> 133 us
    all_to_all x3, waiting for transfers between devices: 44.4 us -> 37.5 us  [exchange(): return lax.all_to_all(parts, axes, split_axis=0, concat_axis=0, tiled=True)]
    all_to_all x4, blocking collectives: 130 us -> 133 us  [exchange(): return lax.all_to_all(parts, axes, split_axis=0, concat_axis=0, tiled=True)]
where the time goes in v6:
time: 219 us; the launch traced here: 218 us
  blocking collectives  133 us (61%)
  waiting for transfers between devices  37.5 us (17%)
  starting transfers between devices  14.7 us (7%)
  between operations  14.2 us (6%)
  local copies, waits for them, and re-layouts  6.78 us (3%)
  matrix products  4.81 us (2%)
  other arithmetic  4.63 us (2%)
  Pallas kernels  2.86 us (1%)
    all_to_all x4, blocking collectives, exchange(): return lax.all_to_all(parts, axes, split_axis=0, concat_axis=0, tiled=True)  133 us
    all_to_all x3, waiting for transfers between devices, exchange(): return lax.all_to_all(parts, axes, split_axis=0, concat_axis=0, tiled=True)  37.5 us
    all_to_all x3, starting transfers between devices, exchange(): return lax.all_to_all(parts, axes, split_axis=0, concat_axis=0, tiled=True)  14.7 us
    dot_general x11, matrix products, dot(): return lax.dot_general(a, b, (dims, ((), ())), preferred_element_type=F32)  4.46 us
  transfers between devices with their start and end apart: 5, of which 3 were waited for; matrix products, arithmetic and copies ran while one was open for 4% of the time, Pallas kernels for 1%

profile of v6, /device:TPU:1, one launch (start us, length us, event | category | flops | bytes accessed | tf_op | source)
XLA Modules:
  0.0 218.2 jit_solution(3292072222331052836)
XLA Ops:
  7.2 0.0 copy-start
  7.2 0.0 copy-start.3
  7.2 0.0 copy-start.4
  7.2 0.0 all-gather.3.cloned.1.call-start
  7.2 2.0 pad_maximum_fusion.1
  9.2 0.0 all-gather.3.cloned.1.call-update
  9.2 0.0 copy-done
  9.2 0.0 copy-done.3
  9.3 0.3 fusion.31
  9.6 0.2 fusion.22
  9.8 0.0 copy-done.4
  9.8 0.2 fusion.3
  10.0 0.2 fusion.2
  10.3 0.2 copy.24
  10.5 0.1 reshape.47
  10.6 64.5 %all_to_all.35 = bf16[32,4,768]{2,1,0:T(4,128)(2,1)S(1)} all-to-all(bf16[32,4,768]{2,1,0:T(4,128)(2,1)S(1)} %reshape.47), channel_id=1, replica_groups=mesh['x'=4,'y'=4,'zh'=16,'zl'=2,'c'=2] {'zh','zl'}, dimensions={0} | all-to-all | bytes 393216 | tf_op jit(solution)/shard_map/all_to_all | solution.py:20
  75.1 1.0 broadcast_in_dim.12
  76.1 6.9 %all-to-all-start.1 = ((bf16[8,2,32,768]{3,2,1,0:T(8,128)(2,1)}), bf16[8,2,32,768]{3,2,1,0:T(8,128)(2,1)S(1)}, u32[]{:S(2)}, u32[]{:S(2)}) async-start(bf16[8,2,32,768]{3,2,1,0:T(8,128)(2,1)} %bitcast.6), calls=%async_computation.1 | async-start | bytes 1572864 | tf_op jit(solution)/shard_map/all_to_all | solution.py:20
  82.9 0.0 all-gather.3.cloned.1.call-done
  82.9 2.8 %fusion.32 = (bf16[4,192,768]{2,1,0:T(8,128)(2,1)}, bf16[4,192,768]{2,1,0:T(8,128)(2,1)S(1)}) fusion(bf16[4,384,768]{2,1,0:T(8,128)(2,1)} %bitcast.93), kind=kLoop, calls=%fused_computation.51 | loop fusion | bytes 4718592 | tf_op jit(solution)/shard_map/slice | solution.py:96
  85.7 9.5 %all-to-all-done.1 = bf16[8,2,32,768]{3,2,1,0:T(8,128)(2,1)S(1)} async-done(((bf16[8,2,32,768]{3,2,1,0:T(8,128)(2,1)}), bf16[8,2,32,768]{3,2,1,0:T(8,128)(2,1)S(1)}, u32[]{:S(2)}, u32[]{:S(2)}) %all-to-all-start.1) | async-done | bytes 786464 | tf_op jit(solution)/shard_map/all_to_all | solution.py:20
  95.2 0.1 fusion.33
  95.3 0.0 copy-start.1
  95.3 0.5 multiply_convert_fusion
  95.8 0.7 copy-done.1
  96.6 0.5 convolution_convert_fusion.1
  97.0 0.6 fusion.pre_ref
  97.6 0.5 convolution_convert_fusion
  98.1 1.0 pad_maximum_fusion
  99.1 4.3 %all-to-all-start.2 = ((bf16[8,2,32,768]{3,2,1,0:T(8,128)(2,1)}), bf16[8,2,32,768]{3,2,1,0:T(8,128)(2,1)S(1)}, u32[]{:S(2)}, u32[]{:S(2)}) async-start(bf16[8,2,32,768]{3,2,1,0:T(8,128)(2,1)} %pad_maximum_fusion), calls=%async_computation.2 | async-start | bytes 1572864 | tf_op jit(solution)/shard_map/all_to_all | solution.py:20
  103.4 0.0 reduce-scatter.2.cloned.1.call-start
  103.4 2.9 %shard_map.84 = bf16[4,384,768]{2,1,0:T(8,128)(2,1)} custom-call(bf16[256,768]{1,0:T(8,128)(2,1)S(1)} %bitcast.85, bf16[256,768]{1,0:T(8,128)(2,1)S(1)} %bitcast.87, bf16[256,768]{1,0:T(8,128)(2,1)S(1)} %get-tuple-element.43.act_ref, bf16[256,768]{1,0:T(8,128)(2,1)S(1)} %fusion.pre_ref), custom_call_target="tpu_custom_call" | custom-call | flops 603979776 | bytes 3932160 | tf_op jit(solution)/shard_map/pallas_call | solution.py:59
  106.3 9.4 %all-to-all-done.2 = bf16[8,2,32,768]{3,2,1,0:T(8,128)(2,1)S(1)} async-done(((bf16[8,2,32,768]{3,2,1,0:T(8,128)(2,1)}), bf16[8,2,32,768]{3,2,1,0:T(8,128)(2,1)S(1)}, u32[]{:S(2)}, u32[]{:S(2)}) %all-to-all-start.2) | async-done | bytes 786464 | tf_op jit(solution)/shard_map/all_to_all | solution.py:20
  115.7 0.0 reduce-scatter.2.cloned.1.call-update
  115.7 0.1 reduce_sum.74
  115.9 0.2 copy.30
  116.0 38.4 %all_to_all.36 = bf16[32,4,768]{2,1,0:T(4,128)(2,1)S(1)} all-to-all(bf16[32,4,768]{2,1,0:T(4,128)(2,1)S(1)} %copy.30), channel_id=1, replica_groups=mesh['x'=4,'y'=4,'zh'=16,'zl'=2,'c'=2] {'zh','zl'}, dimensions={0} | all-to-all | bytes 393216 | tf_op jit(solution)/shard_map/all_to_all | solution.py:20
  154.4 0.1 reshape.54
  154.5 0.3 fusion.34
  154.8 0.2 convolution_bitcast_fusion
  155.0 0.3 multiply_reduce_fusion.1
  155.3 0.1 add_convert_fusion
  155.4 0.2 convolution_convert_fusion.2
  155.6 16.1 %all_to_all.37 = bf16[64,2,384]{2,1,0:T(2,128)(2,1)S(1)} all-to-all(bf16[64,2,384]{2,1,0:T(2,128)(2,1)S(1)} %reshape.55), channel_id=1, replica_groups=mesh['x'=4,'y'=4,'zh'=16,'zl'=2,'c'=2] {'x','y','zl','c'}, dimensions={0} | all-to-all | bytes 196608 | tf_op jit(solution)/shard_map/all_to_all | solution.py:20
  171.7 0.1 reduce_sum.77
  171.8 0.0 reduce-scatter.2.cloned.1.call-done
  171.8 0.0 copy-start.2
  171.9 0.6 broadcast_in_dim.13
  172.5 3.5 %all-to-all-start.5 = ((bf16[16,2,384]{2,1,0:T(2,128)(2,1)}), bf16[16,2,384]{2,1,0:T(2,128)(2,1)S(1)}, u32[]{:S(2)}, u32[]{:S(2)}) async-start(bf16[16,2,384]{2,1,0:T(2,128)(2,1)} %broadcast_in_dim.13), calls=%async_computation.6 | async-start | bytes 49152 | tf_op jit(solution)/shard_map/all_to_all | solution.py:20
  176.0 0.3 fusion.35
  176.2 0.0 copy-done.2
  176.3 1.1 slice_convert_fusion
  177.3 1.1 fusion.1
  178.4 18.5 %all-to-all-done.5 = bf16[16,2,384]{2,1,0:T(2,128)(2,1)S(1)} async-done(((bf16[16,2,384]{2,1,0:T(2,128)(2,1)}), bf16[16,2,384]{2,1,0:T(2,128)(2,1)S(1)}, u32[]{:S(2)}, u32[]{:S(2)}) %all-to-all-start.5) | async-done | bytes 24608 | tf_op jit(solution)/shard_map/all_to_all | solution.py:20
  197.0 0.1 broadcast_in_dim.15
  197.1 13.6 %all_to_all.38 = bf16[64,2,384]{2,1,0:T(2,128)(2,1)S(1)} all-to-all(bf16[64,2,384]{2,1,0:T(2,128)(2,1)S(1)} %broadcast_in_dim.15), channel_id=1, replica_groups=mesh['x'=4,'y'=4,'zh'=16,'zl'=2,'c'=2] {'x','y','zl','c'}, dimensions={0} | all-to-all | bytes 196608 | tf_op jit(solution)/shard_map/all_to_all | solution.py:20
  210.6 0.7 copy.36
  (4 shorter events, 0.1 us)
Async XLA Ops:
  7.2 2.1 copy-start
  7.2 2.1 copy-start.3
  7.2 2.6 %copy-start.4 = (bf16[1,196,768]{2,1,0:T(8,128)(2,1)S(1)}, bf16[1,196,768]{2,1,0:T(8,128)(2,1)}, u32[]{:S(2)}) copy-start(bf16[1,196,768]{2,1,0:T(8,128)(2,1)} %param.9) | copy-start | bytes 903172
  7.2 75.7 %all-gather.3.cloned.1.call-start = ((), (), s32[]{:S(2)}) async-start(), calls=%async_computation.9 | async-start | bytes 2949120 | tf_op jit(solution)/shard_map/all_gather | solution.py:82
  76.1 19.2 %all-to-all-start.1 = ((bf16[8,2,32,768]{3,2,1,0:T(8,128)(2,1)}), bf16[8,2,32,768]{3,2,1,0:T(8,128)(2,1)S(1)}, u32[]{:S(2)}, u32[]{:S(2)}) async-start(bf16[8,2,32,768]{3,2,1,0:T(8,128)(2,1)} %bitcast.6), calls=%async_computation.1 | async-start | bytes 1572864 | tf_op jit(solution)/shard_map/all_to_all | solution.py:20
  95.3 1.3 copy-start.1
  99.1 16.6 %all-to-all-start.2 = ((bf16[8,2,32,768]{3,2,1,0:T(8,128)(2,1)}), bf16[8,2,32,768]{3,2,1,0:T(8,128)(2,1)S(1)}, u32[]{:S(2)}, u32[]{:S(2)}) async-start(bf16[8,2,32,768]{3,2,1,0:T(8,128)(2,1)} %pad_maximum_fusion), calls=%async_computation.2 | async-start | bytes 1572864 | tf_op jit(solution)/shard_map/all_to_all | solution.py:20
  103.4 68.4 %reduce-scatter.2.cloned.1.call-start = ((), (), s32[]{:S(2)}) async-start(), calls=%async_computation.8 | async-start | bytes 2949120 | tf_op jit(solution)/shard_map/reduce_scatter | solution.py:112
  171.8 4.4 %copy-start.2 = (bf16[1,384,768]{2,1,0:T(8,128)(2,1)S(1)}, bf16[1,384,768]{2,1,0:T(8,128)(2,1)}, u32[]{:S(2)}) copy-start(bf16[1,384,768]{2,1,0:T(8,128)(2,1)} %reduce-scatter.2.cloned.1.call-done) | copy-start | bytes 1769476
  172.5 24.5 %all-to-all-start.5 = ((bf16[16,2,384]{2,1,0:T(2,128)(2,1)}), bf16[16,2,384]{2,1,0:T(2,128)(2,1)S(1)}, u32[]{:S(2)}, u32[]{:S(2)}) async-start(bf16[16,2,384]{2,1,0:T(2,128)(2,1)} %broadcast_in_dim.13), calls=%async_computation.6 | async-start | bytes 49152 | tf_op jit(solution)/shard_map/all_to_all | solution.py:20
Sparse Core Ops, SparseCore 0:
  11.3 59.2 all-gather.2
  115.9 29.2 reduce-scatter.1

commit v7 on v6

--- a/solution.py
+++ b/solution.py
@@ -13,11 +13,14 @@
 ALL = ("x", "y", "zh", "zl", "c")
 EXPERT = ("zh", "zl", "c")
 BOX = ("x", "y", "zl", "c")
+CHIPS = ("x", "y", "c")
 VMEM_BYTES = 16 * 1024 * 1024
 
 
-def exchange(parts, axes):
-    return lax.all_to_all(parts, axes, split_axis=0, concat_axis=0, tiled=True)
+def exchange(parts, axes, groups=None):
+    return lax.all_to_all(
+        parts, axes, split_axis=0, concat_axis=0, tiled=True, axis_index_groups=groups
+    )
 
 
 def spread(mine, axes, count):
@@ -78,8 +81,12 @@
     block = w_out.shape[1]
     box = nx * ny * nl * nc
 
+    at = np.arange(nx * ny * nc).reshape(nx, ny, nc)
+    row_groups = [*at[:, :, 0].tolist(), *at[:, :, 1].T.tolist()]
+    unit_groups = [*at[:, :, 0].T.tolist(), *at[:, :, 1].tolist()]
+
     weights = jnp.concatenate([w_in[0].T, w_out[0]], axis=0)
-    gathered = lax.all_gather(weights, "x", axis=0, tiled=False)
+    gathered = lax.all_gather(weights, CHIPS, axis=0, tiled=False, axis_index_groups=unit_groups)
 
     logits = jnp.dot(tok, router, preferred_element_type=F32)
     dispatch = jax.nn.softmax(logits, axis=0)
@@ -88,10 +95,9 @@
     combine_b = combine.astype(BF)
     slots = dot(dispatch_b, tok, ((0,), (0,))).astype(BF)
     slot_grad = dot(combine_b, og, ((0,), (0,))).astype(BF)
-    sent = jnp.stack([slots, slot_grad], axis=1).reshape(nz, nc * 2, width)
-    mine = exchange(sent, Z).reshape(nz, nc, 2, width).transpose(1, 2, 0, 3)
-    copies = jnp.broadcast_to(mine[None], (ny, nc, 2, nz, width))
-    rows = exchange(copies.reshape(ny * nc, 2, nz, width), ("y", "c"))
+    mine = exchange(jnp.stack([slots, slot_grad], axis=1), EXPERT)
+    pair = jnp.stack([mine[:, 0], mine[:, 1]], axis=0)
+    rows = exchange(jnp.broadcast_to(pair[None], (ny, *pair.shape)), CHIPS, row_groups)
     first = gathered[:, :block].reshape(nx * block, width)
     second = gathered[:, block:].reshape(nx * block, width)
     rows, first, second = lax.optimization_barrier((rows, first, second))
@@ -104,16 +110,17 @@
     pre_grad = (act_grad * gelu_slope(hidden)).astype(BF)
     partial_out = dot(act, second, ((1,), (0,))).astype(BF)
     partial_in = dot(pre_grad, first, ((1,), (0,))).astype(BF)
-    shape = (ny * nc, nz, width)
+    shape = (ny, experts, width)
     partial = jnp.stack([partial_out.reshape(shape), partial_in.reshape(shape)], axis=1)
-    parts_of_mine = exchange(partial, ("y", "c"))
+    parts_of_mine = exchange(partial, CHIPS, row_groups)
     parts = weight_parts(rows_in, rows_grad, act, pre_grad, nx)
     parts_of_mine, parts = lax.optimization_barrier((parts_of_mine, parts))
-    grads = lax.psum_scatter(parts, "x", scatter_dimension=0, tiled=False)
+    grads = lax.psum_scatter(
+        parts, CHIPS, scatter_dimension=0, tiled=False, axis_index_groups=unit_groups
+    )
 
-    summed = parts_of_mine.reshape(ny, nc, 2, nz, width).astype(F32).sum(axis=0).astype(BF)
-    back = exchange(summed.transpose(2, 0, 1, 3).reshape(nz, nc * 2, width), Z)
-    back = back.reshape(experts, 2, width)
+    summed = parts_of_mine.astype(F32).sum(axis=0).astype(BF)
+    back = exchange(jnp.stack([summed[0], summed[1]], axis=1), EXPERT)
     expert_out, slot_in_grad = back[:, 0], back[:, 1]
 
     combine_dot = dot(og, expert_out, ((1,), (1,)))

time: 219 us -> 214 us (0.977)
  waiting for transfers between devices: 37.5 us -> 29.5 us
  blocking collectives: 133 us -> 140 us
  starting transfers between devices: 14.7 us -> 11.1 us
    all_to_all x3, waiting for transfers between devices: 37.5 us -> 29.5 us  [exchange(): lax.all_to_all(parts, axes, split_axis=0, concat_axis=0, tiled=True, axis...]
    all_to_all x4, blocking collectives: 133 us -> 140 us  [exchange(): lax.all_to_all(parts, axes, split_axis=0, concat_axis=0, tiled=True, axis...]
    all_to_all x3, starting transfers between devices: 14.7 us -> 11 us  [exchange(): lax.all_to_all(parts, axes, split_axis=0, concat_axis=0, tiled=True, axis...]
where the time goes in v7:
time: 214 us
  blocking collectives  140 us (65%)
  waiting for transfers between devices  29.5 us (14%)
  between operations  14.3 us (7%)
  starting transfers between devices  11.1 us (5%)
  local copies, waits for them, and re-layouts  6.95 us (3%)
  matrix products  4.8 us (2%)
  other arithmetic  4.67 us (2%)
  Pallas kernels  2.88 us (1%)
    all_to_all x4, blocking collectives, exchange(): lax.all_to_all(parts, axes, split_axis=0, concat_axis=0, tiled=True, axis...  140 us
    all_to_all x3, waiting for transfers between devices, exchange(): lax.all_to_all(parts, axes, split_axis=0, concat_axis=0, tiled=True, axis...  29.5 us
    all_to_all x3, starting transfers between devices, exchange(): lax.all_to_all(parts, axes, split_axis=0, concat_axis=0, tiled=True, axis...  11 us
    dot_general x11, matrix products, dot(): return lax.dot_general(a, b, (dims, ((), ())), preferred_element_type=F32)  4.46 us
  transfers between devices with their start and end apart: 5, of which 3 were waited for; matrix products, arithmetic and copies ran while one was open for 4% of the time, Pallas kernels for 1%

profile of v7, /device:TPU:1, one launch (start us, length us, event | category | flops | bytes accessed | tf_op | source)
XLA Modules:
  0.0 213.8 jit_solution(4861822810875149025)
XLA Ops:
  7.2 0.0 copy-start
  7.2 0.0 copy-start.3
  7.2 0.0 copy-start.4
  7.2 0.0 all-gather.3.cloned.1.call-start
  7.2 2.0 pad_maximum_fusion.1
  9.2 0.0 all-gather.3.cloned.1.call-update
  9.2 0.0 copy-done
  9.2 0.0 copy-done.3
  9.3 0.3 fusion.25
  9.6 0.2 fusion.18
  9.8 0.0 copy-done.4
  9.8 0.2 fusion.3
  10.0 0.2 fusion.2
  10.3 0.2 copy.14
  10.5 66.8 %all_to_all.35 = bf16[64,2,768]{2,1,0:T(2,128)(2,1)S(1)} all-to-all(bf16[64,2,768]{2,1,0:T(2,128)(2,1)S(1)} %copy.14), channel_id=1, replica_groups=mesh['x'=4,'y'=4,'zh'=16,'zl'=2,'c'=2] {'zh','zl','c'}, dimensions={0} | all-to-all | bytes 393216 | tf_op jit(solution)/shard_map/all_to_all | solution.py:21
  77.3 0.3 fusion.29
  77.7 0.9 broadcast_in_dim.12
  78.6 4.0 %all-to-all-start.1 = ((bf16[4,2,64,768]{3,2,1,0:T(8,128)(2,1)}), bf16[4,2,64,768]{3,2,1,0:T(8,128)(2,1)S(1)}, u32[]{:S(2)}, u32[]{:S(2)}) async-start(bf16[4,2,64,768]{3,2,1,0:T(8,128)(2,1)} %broadcast_in_dim.12), calls=%async_computation.1 | async-start | bytes 1572864 | tf_op jit(solution)/shard_map/all_to_all | solution.py:21
  82.6 0.0 all-gather.3.cloned.1.call-done
  82.6 2.8 %fusion.26 = (bf16[4,192,768]{2,1,0:T(8,128)(2,1)}, bf16[4,192,768]{2,1,0:T(8,128)(2,1)S(1)}) fusion(bf16[4,384,768]{2,1,0:T(8,128)(2,1)} %bitcast.89), kind=kLoop, calls=%fused_computation.53 | loop fusion | bytes 4718592 | tf_op jit(solution)/shard_map/slice | solution.py:102
  85.4 5.5 %all-to-all-done.1 = bf16[4,2,64,768]{3,2,1,0:T(8,128)(2,1)S(1)} async-done(((bf16[4,2,64,768]{3,2,1,0:T(8,128)(2,1)}), bf16[4,2,64,768]{3,2,1,0:T(8,128)(2,1)S(1)}, u32[]{:S(2)}, u32[]{:S(2)}) %all-to-all-start.1) | async-done | bytes 786464 | tf_op jit(solution)/shard_map/all_to_all | solution.py:21
  90.9 0.1 fusion.27
  91.0 0.0 copy-start.1
  91.0 0.5 multiply_convert_fusion
  91.5 0.7 copy-done.1
  92.3 0.5 convolution_convert_fusion.1
  92.8 0.6 fusion.pre_ref
  93.3 0.5 convolution_convert_fusion
  93.8 1.0 pad_maximum_fusion
  94.8 3.5 %all-to-all-start.2 = ((bf16[4,2,64,768]{3,2,1,0:T(8,128)(2,1)}), bf16[4,2,64,768]{3,2,1,0:T(8,128)(2,1)S(1)}, u32[]{:S(2)}, u32[]{:S(2)}) async-start(bf16[4,2,64,768]{3,2,1,0:T(8,128)(2,1)} %pad_maximum_fusion), calls=%async_computation.2 | async-start | bytes 1572864 | tf_op jit(solution)/shard_map/all_to_all | solution.py:21
  98.3 0.0 reduce-scatter.2.cloned.1.call-start
  98.3 2.9 %shard_map.84 = bf16[4,384,768]{2,1,0:T(8,128)(2,1)} custom-call(bf16[256,768]{1,0:T(8,128)(2,1)S(1)} %bitcast.82, bf16[256,768]{1,0:T(8,128)(2,1)S(1)} %bitcast.84, bf16[256,768]{1,0:T(8,128)(2,1)S(1)} %get-tuple-element.47.act_ref, bf16[256,768]{1,0:T(8,128)(2,1)S(1)} %fusion.pre_ref), custom_call_target="tpu_custom_call" | custom-call | flops 603979776 | bytes 3932160 | tf_op jit(solution)/shard_map/pallas_call | solution.py:62
  101.2 5.4 %all-to-all-done.2 = bf16[4,2,64,768]{3,2,1,0:T(8,128)(2,1)S(1)} async-done(((bf16[4,2,64,768]{3,2,1,0:T(8,128)(2,1)}), bf16[4,2,64,768]{3,2,1,0:T(8,128)(2,1)S(1)}, u32[]{:S(2)}, u32[]{:S(2)}) %all-to-all-start.2) | async-done | bytes 786464 | tf_op jit(solution)/shard_map/all_to_all | solution.py:21
  106.6 0.0 reduce-scatter.2.cloned.1.call-update
  106.6 0.1 reduce_sum.74
  106.8 0.2 copy.19
  107.0 44.4 %all_to_all.36 = bf16[64,2,768]{2,1,0:T(2,128)(2,1)S(1)} all-to-all(bf16[64,2,768]{2,1,0:T(2,128)(2,1)S(1)} %copy.19), channel_id=1, replica_groups=mesh['x'=4,'y'=4,'zh'=16,'zl'=2,'c'=2] {'zh','zl','c'}, dimensions={0} | all-to-all | bytes 393216 | tf_op jit(solution)/shard_map/all_to_all | solution.py:21
  151.4 0.3 fusion.28
  151.6 0.2 convolution_bitcast_fusion
  151.9 0.3 multiply_reduce_fusion.1
  152.1 0.1 add_convert_fusion
  152.2 0.2 convolution_convert_fusion.2
  152.5 14.8 %all_to_all.37 = bf16[64,2,384]{2,1,0:T(2,128)(2,1)S(1)} all-to-all(bf16[64,2,384]{2,1,0:T(2,128)(2,1)S(1)} %reshape.31), channel_id=1, replica_groups=mesh['x'=4,'y'=4,'zh'=16,'zl'=2,'c'=2] {'x','y','zl','c'}, dimensions={0} | all-to-all | bytes 196608 | tf_op jit(solution)/shard_map/all_to_all | solution.py:21
  167.3 0.1 reduce_sum.77
  167.4 0.0 reduce-scatter.2.cloned.1.call-done
  167.4 0.0 copy-start.2
  167.5 0.6 broadcast_in_dim.13
  168.1 3.5 %all-to-all-start.5 = ((bf16[16,2,384]{2,1,0:T(2,128)(2,1)}), bf16[16,2,384]{2,1,0:T(2,128)(2,1)S(1)}, u32[]{:S(2)}, u32[]{:S(2)}) async-start(bf16[16,2,384]{2,1,0:T(2,128)(2,1)} %broadcast_in_dim.13), calls=%async_computation.6 | async-start | bytes 49152 | tf_op jit(solution)/shard_map/all_to_all | solution.py:21
  171.6 0.3 fusion.30
  171.8 0.0 copy-done.2
  171.9 1.1 slice_convert_fusion
  172.9 1.1 fusion.1
  174.0 18.5 %all-to-all-done.5 = bf16[16,2,384]{2,1,0:T(2,128)(2,1)S(1)} async-done(((bf16[16,2,384]{2,1,0:T(2,128)(2,1)}), bf16[16,2,384]{2,1,0:T(2,128)(2,1)S(1)}, u32[]{:S(2)}, u32[]{:S(2)}) %all-to-all-start.5) | async-done | bytes 24608 | tf_op jit(solution)/shard_map/all_to_all | solution.py:21
  192.6 0.1 broadcast_in_dim.15
  192.7 13.6 %all_to_all.38 = bf16[64,2,384]{2,1,0:T(2,128)(2,1)S(1)} all-to-all(bf16[64,2,384]{2,1,0:T(2,128)(2,1)S(1)} %broadcast_in_dim.15), channel_id=1, replica_groups=mesh['x'=4,'y'=4,'zh'=16,'zl'=2,'c'=2] {'x','y','zl','c'}, dimensions={0} | all-to-all | bytes 196608 | tf_op jit(solution)/shard_map/all_to_all | solution.py:21
  206.2 0.7 copy.26
  (7 shorter events, 0.2 us)
Async XLA Ops:
  7.2 2.1 copy-start
  7.2 2.1 copy-start.3
  7.2 2.6 %copy-start.4 = (bf16[1,196,768]{2,1,0:T(8,128)(2,1)S(1)}, bf16[1,196,768]{2,1,0:T(8,128)(2,1)}, u32[]{:S(2)}) copy-start(bf16[1,196,768]{2,1,0:T(8,128)(2,1)} %param.9) | copy-start | bytes 903172
  7.2 75.4 %all-gather.3.cloned.1.call-start = ((), (), s32[]{:S(2)}) async-start(), calls=%async_computation.9 | async-start | bytes 2949120 | tf_op jit(solution)/shard_map/all_gather | solution.py:89
  78.6 12.4 %all-to-all-start.1 = ((bf16[4,2,64,768]{3,2,1,0:T(8,128)(2,1)}), bf16[4,2,64,768]{3,2,1,0:T(8,128)(2,1)S(1)}, u32[]{:S(2)}, u32[]{:S(2)}) async-start(bf16[4,2,64,768]{3,2,1,0:T(8,128)(2,1)} %broadcast_in_dim.12), calls=%async_computation.1 | async-start | bytes 1572864 | tf_op jit(solution)/shard_map/all_to_all | solution.py:21
  91.0 1.3 copy-start.1
  94.8 11.8 %all-to-all-start.2 = ((bf16[4,2,64,768]{3,2,1,0:T(8,128)(2,1)}), bf16[4,2,64,768]{3,2,1,0:T(8,128)(2,1)S(1)}, u32[]{:S(2)}, u32[]{:S(2)}) async-start(bf16[4,2,64,768]{3,2,1,0:T(8,128)(2,1)} %pad_maximum_fusion), calls=%async_computation.2 | async-start | bytes 1572864 | tf_op jit(solution)/shard_map/all_to_all | solution.py:21
  98.3 69.1 %reduce-scatter.2.cloned.1.call-start = ((), (), s32[]{:S(2)}) async-start(), calls=%async_computation.8 | async-start | bytes 2949120 | tf_op jit(solution)/shard_map/reduce_scatter | solution.py:118
  167.4 4.4 %copy-start.2 = (bf16[1,384,768]{2,1,0:T(8,128)(2,1)S(1)}, bf16[1,384,768]{2,1,0:T(8,128)(2,1)}, u32[]{:S(2)}) copy-start(bf16[1,384,768]{2,1,0:T(8,128)(2,1)} %reduce-scatter.2.cloned.1.call-done) | copy-start | bytes 1769476
  168.1 24.5 %all-to-all-start.5 = ((bf16[16,2,384]{2,1,0:T(2,128)(2,1)}), bf16[16,2,384]{2,1,0:T(2,128)(2,1)S(1)}, u32[]{:S(2)}, u32[]{:S(2)}) async-start(bf16[16,2,384]{2,1,0:T(2,128)(2,1)} %broadcast_in_dim.13), calls=%async_computation.6 | async-start | bytes 49152 | tf_op jit(solution)/shard_map/all_to_all | solution.py:21
Sparse Core Ops, SparseCore 0:
  11.3 50.4 all-gather.2
  106.7 24.1 reduce-scatter.1

commit v8 on v7

--- a/solution.py
+++ b/solution.py
@@ -98,9 +98,9 @@
     mine = exchange(jnp.stack([slots, slot_grad], axis=1), EXPERT)
     pair = jnp.stack([mine[:, 0], mine[:, 1]], axis=0)
     rows = exchange(jnp.broadcast_to(pair[None], (ny, *pair.shape)), CHIPS, row_groups)
+    rows, gathered = lax.optimization_barrier((rows, gathered))
     first = gathered[:, :block].reshape(nx * block, width)
     second = gathered[:, block:].reshape(nx * block, width)
-    rows, first, second = lax.optimization_barrier((rows, first, second))
     rows_in = rows[:, 0].reshape(ny * experts, width)
     rows_grad = rows[:, 1].reshape(ny * experts, width)
 

time: 214 us -> 214 us (level)
  blocking collectives: 140 us -> 152 us
  waiting for transfers between devices: 29.5 us -> 24 us
  starting transfers between devices: 11.1 us -> 7.07 us
  local copies, waits for them, and re-layouts: 6.95 us -> 4.32 us
    all_to_all x4 -> x5, blocking collectives: 140 us -> 152 us  [exchange(): lax.all_to_all(parts, axes, split_axis=0, concat_axis=0, tiled=True, axis...]
    all_to_all x3 -> x2, waiting for transfers between devices: 29.5 us -> 23.9 us  [exchange(): lax.all_to_all(parts, axes, split_axis=0, concat_axis=0, tiled=True, axis...]
    all_to_all x3 -> x2, starting transfers between devices: 11 us -> 6.99 us  [exchange(): lax.all_to_all(parts, axes, split_axis=0, concat_axis=0, tiled=True, axis...]
  transfers between devices with their start and end apart: 5 -> 4, of which waited for: 3 -> 2; matrix products, arithmetic and copies ran while one was open for 4% -> 3% of each run, Pallas kernels for 1% -> 1%
where the time goes in v8:
time: 214 us
  blocking collectives  152 us (71%)
  waiting for transfers between devices  24 us (11%)
  between operations  14.3 us (7%)
  starting transfers between devices  7.07 us (3%)
  matrix products  4.85 us (2%)
  other arithmetic  4.67 us (2%)
  local copies, waits for them, and re-layouts  4.32 us (2%)
  Pallas kernels  2.86 us (1%)
    all_to_all x5, blocking collectives, exchange(): lax.all_to_all(parts, axes, split_axis=0, concat_axis=0, tiled=True, axis...  152 us
    all_to_all x2, waiting for transfers between devices, exchange(): lax.all_to_all(parts, axes, split_axis=0, concat_axis=0, tiled=True, axis...  23.9 us
    all_to_all x2, starting transfers between devices, exchange(): lax.all_to_all(parts, axes, split_axis=0, concat_axis=0, tiled=True, axis...  6.99 us
    dot_general x11, matrix products, dot(): return lax.dot_general(a, b, (dims, ((), ())), preferred_element_type=F32)  4.5 us
  transfers between devices with their start and end apart: 4, of which 2 were waited for; matrix products, arithmetic and copies ran while one was open for 3% of the time, Pallas kernels for 1%

profile of v8, /device:TPU:1, one launch (start us, length us, event | category | flops | bytes accessed | tf_op | source)
XLA Modules:
  0.0 213.8 jit_solution(4450742383192755062)
XLA Ops:
  7.2 0.0 copy-start
  7.2 0.0 copy-start.2
  7.2 0.0 copy-start.3
  7.2 0.0 all-gather.3.cloned.1.call-start
  7.2 2.0 pad_maximum_fusion.1
  9.2 0.0 all-gather.3.cloned.1.call-update
  9.2 0.0 copy-done
  9.2 0.0 copy-done.2
  9.3 0.3 fusion.25
  9.6 0.2 fusion.18
  9.8 0.0 copy-done.3
  9.8 0.2 fusion.3
  10.0 0.2 fusion.2
  10.3 0.2 copy.14
  10.5 66.8 %all_to_all.35 = bf16[64,2,768]{2,1,0:T(2,128)(2,1)S(1)} all-to-all(bf16[64,2,768]{2,1,0:T(2,128)(2,1)S(1)} %copy.14), channel_id=1, replica_groups=mesh['x'=4,'y'=4,'zh'=16,'zl'=2,'c'=2] {'zh','zl','c'}, dimensions={0} | all-to-all | bytes 393216 | tf_op jit(solution)/shard_map/all_to_all | solution.py:21
  77.3 0.3 fusion.29
  77.7 0.1 broadcast_in_dim.12
  77.7 12.4 %all_to_all.36 = bf16[4,2,64,768]{3,2,1,0:T(8,128)(2,1)S(1)} all-to-all(bf16[4,2,64,768]{3,2,1,0:T(8,128)(2,1)S(1)} %broadcast_in_dim.12), channel_id=1, replica_groups={{0,64,128,192},{256,320,384,448},{512,576,640,704},{768,832,896,960},{1..., dimensions={0} | all-to-all | bytes 1572864 | tf_op jit(solution)/shard_map/all_to_all | solution.py:21
  90.2 0.0 all-gather.3.cloned.1.call-done
  90.2 0.1 fusion.27
  90.2 1.8 fusion.26
  92.0 0.5 multiply_convert_fusion
  92.6 0.5 convolution_convert_fusion.1
  93.1 0.6 fusion.pre_ref
  93.6 0.5 convolution_convert_fusion
  94.1 1.0 pad_maximum_fusion
  95.1 3.5 %all-to-all-start.2 = ((bf16[4,2,64,768]{3,2,1,0:T(8,128)(2,1)}), bf16[4,2,64,768]{3,2,1,0:T(8,128)(2,1)S(1)}, u32[]{:S(2)}, u32[]{:S(2)}) async-start(bf16[4,2,64,768]{3,2,1,0:T(8,128)(2,1)} %pad_maximum_fusion), calls=%async_computation.2 | async-start | bytes 1572864 | tf_op jit(solution)/shard_map/all_to_all | solution.py:21
  98.6 0.0 reduce-scatter.2.cloned.1.call-start
  98.7 2.9 %shard_map.84 = bf16[4,384,768]{2,1,0:T(8,128)(2,1)} custom-call(bf16[256,768]{1,0:T(8,128)(2,1)S(1)} %bitcast.82, bf16[256,768]{1,0:T(8,128)(2,1)S(1)} %bitcast.84, bf16[256,768]{1,0:T(8,128)(2,1)S(1)} %get-tuple-element.45.act_ref, bf16[256,768]{1,0:T(8,128)(2,1)S(1)} %fusion.pre_ref), custom_call_target="tpu_custom_call" | custom-call | flops 603979776 | bytes 3932160 | tf_op jit(solution)/shard_map/pallas_call | solution.py:62
  101.5 5.4 %all-to-all-done.2 = bf16[4,2,64,768]{3,2,1,0:T(8,128)(2,1)S(1)} async-done(((bf16[4,2,64,768]{3,2,1,0:T(8,128)(2,1)}), bf16[4,2,64,768]{3,2,1,0:T(8,128)(2,1)S(1)}, u32[]{:S(2)}, u32[]{:S(2)}) %all-to-all-start.2) | async-done | bytes 786464 | tf_op jit(solution)/shard_map/all_to_all | solution.py:21
  106.9 0.0 reduce-scatter.2.cloned.1.call-update
  106.9 0.1 reduce_sum.74
  107.1 0.2 copy.19
  107.3 44.1 %all_to_all.37 = bf16[64,2,768]{2,1,0:T(2,128)(2,1)S(1)} all-to-all(bf16[64,2,768]{2,1,0:T(2,128)(2,1)S(1)} %copy.19), channel_id=1, replica_groups=mesh['x'=4,'y'=4,'zh'=16,'zl'=2,'c'=2] {'zh','zl','c'}, dimensions={0} | all-to-all | bytes 393216 | tf_op jit(solution)/shard_map/all_to_all | solution.py:21
  151.4 0.3 fusion.28
  151.7 0.2 convolution_bitcast_fusion
  151.9 0.3 multiply_reduce_fusion.1
  152.1 0.1 add_convert_fusion
  152.3 0.2 convolution_convert_fusion.2
  152.5 14.8 %all_to_all.38 = bf16[64,2,384]{2,1,0:T(2,128)(2,1)S(1)} all-to-all(bf16[64,2,384]{2,1,0:T(2,128)(2,1)S(1)} %reshape.31), channel_id=1, replica_groups=mesh['x'=4,'y'=4,'zh'=16,'zl'=2,'c'=2] {'x','y','zl','c'}, dimensions={0} | all-to-all | bytes 196608 | tf_op jit(solution)/shard_map/all_to_all | solution.py:21
  167.3 0.1 reduce_sum.77
  167.4 0.0 reduce-scatter.2.cloned.1.call-done
  167.5 0.0 copy-start.1
  167.5 0.6 broadcast_in_dim.13
  168.1 3.5 %all-to-all-start.5 = ((bf16[16,2,384]{2,1,0:T(2,128)(2,1)}), bf16[16,2,384]{2,1,0:T(2,128)(2,1)S(1)}, u32[]{:S(2)}, u32[]{:S(2)}) async-start(bf16[16,2,384]{2,1,0:T(2,128)(2,1)} %broadcast_in_dim.13), calls=%async_computation.6 | async-start | bytes 49152 | tf_op jit(solution)/shard_map/all_to_all | solution.py:21
  171.6 0.3 fusion.30
  171.9 0.0 copy-done.1
  171.9 1.1 slice_convert_fusion
  173.0 1.1 fusion.1
  174.0 18.5 %all-to-all-done.5 = bf16[16,2,384]{2,1,0:T(2,128)(2,1)S(1)} async-done(((bf16[16,2,384]{2,1,0:T(2,128)(2,1)}), bf16[16,2,384]{2,1,0:T(2,128)(2,1)S(1)}, u32[]{:S(2)}, u32[]{:S(2)}) %all-to-all-start.5) | async-done | bytes 24608 | tf_op jit(solution)/shard_map/all_to_all | solution.py:21
  192.6 0.1 broadcast_in_dim.15
  192.7 13.6 %all_to_all.39 = bf16[64,2,384]{2,1,0:T(2,128)(2,1)S(1)} all-to-all(bf16[64,2,384]{2,1,0:T(2,128)(2,1)S(1)} %broadcast_in_dim.15), channel_id=1, replica_groups=mesh['x'=4,'y'=4,'zh'=16,'zl'=2,'c'=2] {'x','y','zl','c'}, dimensions={0} | all-to-all | bytes 196608 | tf_op jit(solution)/shard_map/all_to_all | solution.py:21
  206.2 0.7 copy.26
  (7 shorter events, 0.2 us)
Async XLA Ops:
  7.2 2.1 copy-start
  7.2 2.1 copy-start.2
  7.2 2.6 %copy-start.3 = (bf16[1,196,768]{2,1,0:T(8,128)(2,1)S(1)}, bf16[1,196,768]{2,1,0:T(8,128)(2,1)}, u32[]{:S(2)}) copy-start(bf16[1,196,768]{2,1,0:T(8,128)(2,1)} %param.9) | copy-start | bytes 903172
  7.2 83.0 %all-gather.3.cloned.1.call-start = ((), (), s32[]{:S(2)}) async-start(), calls=%async_computation.9 | async-start | bytes 2949120 | tf_op jit(solution)/shard_map/all_gather | solution.py:89
  95.1 11.8 %all-to-all-start.2 = ((bf16[4,2,64,768]{3,2,1,0:T(8,128)(2,1)}), bf16[4,2,64,768]{3,2,1,0:T(8,128)(2,1)S(1)}, u32[]{:S(2)}, u32[]{:S(2)}) async-start(bf16[4,2,64,768]{3,2,1,0:T(8,128)(2,1)} %pad_maximum_fusion), calls=%async_computation.2 | async-start | bytes 1572864 | tf_op jit(solution)/shard_map/all_to_all | solution.py:21
  98.6 68.9 %reduce-scatter.2.cloned.1.call-start = ((), (), s32[]{:S(2)}) async-start(), calls=%async_computation.8 | async-start | bytes 2949120 | tf_op jit(solution)/shard_map/reduce_scatter | solution.py:118
  167.5 4.4 %copy-start.1 = (bf16[1,384,768]{2,1,0:T(8,128)(2,1)S(1)}, bf16[1,384,768]{2,1,0:T(8,128)(2,1)}, u32[]{:S(2)}) copy-start(bf16[1,384,768]{2,1,0:T(8,128)(2,1)} %reduce-scatter.2.cloned.1.call-done) | copy-start | bytes 1769476
  168.1 24.5 %all-to-all-start.5 = ((bf16[16,2,384]{2,1,0:T(2,128)(2,1)}), bf16[16,2,384]{2,1,0:T(2,128)(2,1)S(1)}, u32[]{:S(2)}, u32[]{:S(2)}) async-start(bf16[16,2,384]{2,1,0:T(2,128)(2,1)} %broadcast_in_dim.13), calls=%async_computation.6 | async-start | bytes 49152 | tf_op jit(solution)/shard_map/all_to_all | solution.py:21
Sparse Core Ops, SparseCore 0:
  11.3 50.4 all-gather.2
  107.0 23.8 reduce-scatter.1

commit v9 on v8

--- a/solution.py
+++ b/solution.py
@@ -40,6 +40,29 @@
         0.5 * (1.0 + jax.scipy.special.erf(value * 0.7071067811865476))
         + value * jnp.exp(-0.5 * value * value) * 0.3989422804014327
     )
+
+
+def join_kernel(first_ref, second_ref, joint_ref):
+    joint_ref[0] = first_ref[...]
+    joint_ref[1] = second_ref[...]
+
+
+def join(first, second):
+    block, width = first.shape
+    tile = block // 2
+    rows = pl.BlockSpec((tile, width), lambda i: (i, 0))
+    joint = pl.pallas_call(
+        join_kernel,
+        grid=(2,),
+        in_specs=[rows, rows],
+        out_specs=pl.BlockSpec((2, tile, width), lambda i: (0, i, 0)),
+        out_shape=jax.ShapeDtypeStruct((2, block, width), first.dtype),
+        compiler_params=pltpu.CompilerParams(vmem_limit_bytes=60 * 1024 * 1024),
+        cost_estimate=pl.CostEstimate(
+            flops=0, bytes_accessed=8 * first.size, transcendentals=0
+        ),
+    )(first, second)
+    return joint.reshape(2 * block, width)
 
 
 def weight_kernel(rows_in_ref, rows_grad_ref, act_ref, pre_ref, parts_ref):
@@ -85,7 +108,7 @@
     row_groups = [*at[:, :, 0].tolist(), *at[:, :, 1].T.tolist()]
     unit_groups = [*at[:, :, 0].T.tolist(), *at[:, :, 1].tolist()]
 
-    weights = jnp.concatenate([w_in[0].T, w_out[0]], axis=0)
+    weights = join(w_in[0].T, w_out[0])
     gathered = lax.all_gather(weights, CHIPS, axis=0, tiled=False, axis_index_groups=unit_groups)
 
     logits = jnp.dot(tok, router, preferred_element_type=F32)

time: 214 us -> 214 us (level)
  no operation moved by 1% of the time
where the time goes in v9:
time: 214 us
  blocking collectives  152 us (71%)
  waiting for transfers between devices  24 us (11%)
  between operations  14.3 us (7%)
  starting transfers between devices  7.07 us (3%)
  matrix products  4.84 us (2%)
  Pallas kernels  4.79 us (2%)
  local copies, waits for them, and re-layouts  4.32 us (2%)
  other arithmetic  2.71 us (1%)
    all_to_all x5, blocking collectives, exchange(): lax.all_to_all(parts, axes, split_axis=0, concat_axis=0, tiled=True, axis...  152 us
    all_to_all x2, waiting for transfers between devices, exchange(): lax.all_to_all(parts, axes, split_axis=0, concat_axis=0, tiled=True, axis...  23.9 us
    all_to_all x2, starting transfers between devices, exchange(): lax.all_to_all(parts, axes, split_axis=0, concat_axis=0, tiled=True, axis...  6.99 us
    dot_general x11, matrix products, dot(): return lax.dot_general(a, b, (dims, ((), ())), preferred_element_type=F32)  4.5 us
  transfers between devices with their start and end apart: 4, of which 2 were waited for; matrix products, arithmetic and copies ran while one was open for 3% of the time, Pallas kernels for 1%

profile of v9, /device:TPU:1, one launch (start us, length us, event | category | flops | bytes accessed | tf_op | source)
XLA Modules:
  0.0 213.7 jit_solution(15000012544446767597)
XLA Ops:
  7.2 0.0 copy-start
  7.2 0.0 copy-start.2
  7.2 0.0 copy-start.3
  7.2 0.0 all-gather.2.cloned.1.call-start
  7.2 1.9 shard_map.84
  9.2 0.0 all-gather.2.cloned.1.call-update
  9.2 0.0 copy-done
  9.2 0.0 copy-done.2
  9.2 0.3 fusion.25
  9.6 0.2 fusion.18
  9.8 0.0 copy-done.3
  9.8 0.2 fusion.3
  10.0 0.2 fusion.2
  10.2 0.2 copy.14
  10.4 66.8 %all_to_all.35 = bf16[64,2,768]{2,1,0:T(2,128)(2,1)S(1)} all-to-all(bf16[64,2,768]{2,1,0:T(2,128)(2,1)S(1)} %copy.14), channel_id=1, replica_groups=mesh['x'=4,'y'=4,'zh'=16,'zl'=2,'c'=2] {'zh','zl','c'}, dimensions={0} | all-to-all | bytes 393216 | tf_op jit(solution)/shard_map/all_to_all | solution.py:21
  77.3 0.3 fusion.29
  77.6 0.1 broadcast_in_dim.12
  77.7 12.4 %all_to_all.36 = bf16[4,2,64,768]{3,2,1,0:T(8,128)(2,1)S(1)} all-to-all(bf16[4,2,64,768]{3,2,1,0:T(8,128)(2,1)S(1)} %broadcast_in_dim.12), channel_id=1, replica_groups={{0,64,128,192},{256,320,384,448},{512,576,640,704},{768,832,896,960},{1..., dimensions={0} | all-to-all | bytes 1572864 | tf_op jit(solution)/shard_map/all_to_all | solution.py:21
  90.1 0.0 all-gather.2.cloned.1.call-done
  90.1 0.1 fusion.27
  90.2 1.8 fusion.26
  92.0 0.5 multiply_convert_fusion
  92.5 0.5 convolution_convert_fusion.1
  93.0 0.6 fusion.pre_ref
  93.6 0.5 convolution_convert_fusion
  94.1 1.0 pad_maximum_fusion
  95.1 3.5 %all-to-all-start.2 = ((bf16[4,2,64,768]{3,2,1,0:T(8,128)(2,1)}), bf16[4,2,64,768]{3,2,1,0:T(8,128)(2,1)S(1)}, u32[]{:S(2)}, u32[]{:S(2)}) async-start(bf16[4,2,64,768]{3,2,1,0:T(8,128)(2,1)} %pad_maximum_fusion), calls=%async_computation.2 | async-start | bytes 1572864 | tf_op jit(solution)/shard_map/all_to_all | solution.py:21
  98.6 0.0 reduce-scatter.2.cloned.1.call-start
  98.6 2.9 %shard_map.85 = bf16[4,384,768]{2,1,0:T(8,128)(2,1)} custom-call(bf16[256,768]{1,0:T(8,128)(2,1)S(1)} %bitcast.82, bf16[256,768]{1,0:T(8,128)(2,1)S(1)} %bitcast.84, bf16[256,768]{1,0:T(8,128)(2,1)S(1)} %get-tuple-element.45.act_ref, bf16[256,768]{1,0:T(8,128)(2,1)S(1)} %fusion.pre_ref), custom_call_target="tpu_custom_call" | custom-call | flops 603979776 | bytes 3932160 | tf_op jit(solution)/shard_map/pallas_call | solution.py:85
  101.5 5.4 %all-to-all-done.2 = bf16[4,2,64,768]{3,2,1,0:T(8,128)(2,1)S(1)} async-done(((bf16[4,2,64,768]{3,2,1,0:T(8,128)(2,1)}), bf16[4,2,64,768]{3,2,1,0:T(8,128)(2,1)S(1)}, u32[]{:S(2)}, u32[]{:S(2)}) %all-to-all-start.2) | async-done | bytes 786464 | tf_op jit(solution)/shard_map/all_to_all | solution.py:21
  106.9 0.0 reduce-scatter.2.cloned.1.call-update
  106.9 0.1 reduce_sum.74
  107.1 0.2 copy.19
  107.3 44.1 %all_to_all.37 = bf16[64,2,768]{2,1,0:T(2,128)(2,1)S(1)} all-to-all(bf16[64,2,768]{2,1,0:T(2,128)(2,1)S(1)} %copy.19), channel_id=1, replica_groups=mesh['x'=4,'y'=4,'zh'=16,'zl'=2,'c'=2] {'zh','zl','c'}, dimensions={0} | all-to-all | bytes 393216 | tf_op jit(solution)/shard_map/all_to_all | solution.py:21
  151.4 0.3 fusion.28
  151.6 0.2 convolution_bitcast_fusion
  151.9 0.3 multiply_reduce_fusion.1
  152.1 0.1 add_convert_fusion
  152.2 0.2 convolution_convert_fusion.2
  152.5 14.8 %all_to_all.38 = bf16[64,2,384]{2,1,0:T(2,128)(2,1)S(1)} all-to-all(bf16[64,2,384]{2,1,0:T(2,128)(2,1)S(1)} %reshape.31), channel_id=1, replica_groups=mesh['x'=4,'y'=4,'zh'=16,'zl'=2,'c'=2] {'x','y','zl','c'}, dimensions={0} | all-to-all | bytes 196608 | tf_op jit(solution)/shard_map/all_to_all | solution.py:21
  167.3 0.1 reduce_sum.77
  167.4 0.0 reduce-scatter.2.cloned.1.call-done
  167.4 0.0 copy-start.1
  167.4 0.6 broadcast_in_dim.13
  168.1 3.5 %all-to-all-start.5 = ((bf16[16,2,384]{2,1,0:T(2,128)(2,1)}), bf16[16,2,384]{2,1,0:T(2,128)(2,1)S(1)}, u32[]{:S(2)}, u32[]{:S(2)}) async-start(bf16[16,2,384]{2,1,0:T(2,128)(2,1)} %broadcast_in_dim.13), calls=%async_computation.6 | async-start | bytes 49152 | tf_op jit(solution)/shard_map/all_to_all | solution.py:21
  171.6 0.3 fusion.30
  171.8 0.0 copy-done.1
  171.8 1.1 slice_convert_fusion
  172.9 1.1 fusion.1
  174.0 18.5 %all-to-all-done.5 = bf16[16,2,384]{2,1,0:T(2,128)(2,1)S(1)} async-done(((bf16[16,2,384]{2,1,0:T(2,128)(2,1)}), bf16[16,2,384]{2,1,0:T(2,128)(2,1)S(1)}, u32[]{:S(2)}, u32[]{:S(2)}) %all-to-all-start.5) | async-done | bytes 24608 | tf_op jit(solution)/shard_map/all_to_all | solution.py:21
  192.6 0.1 broadcast_in_dim.15
  192.6 13.6 %all_to_all.39 = bf16[64,2,384]{2,1,0:T(2,128)(2,1)S(1)} all-to-all(bf16[64,2,384]{2,1,0:T(2,128)(2,1)S(1)} %broadcast_in_dim.15), channel_id=1, replica_groups=mesh['x'=4,'y'=4,'zh'=16,'zl'=2,'c'=2] {'x','y','zl','c'}, dimensions={0} | all-to-all | bytes 196608 | tf_op jit(solution)/shard_map/all_to_all | solution.py:21
  206.2 0.7 copy.26
  (7 shorter events, 0.2 us)
Async XLA Ops:
  7.2 2.0 copy-start
  7.2 2.0 copy-start.2
  7.2 2.6 %copy-start.3 = (bf16[1,196,768]{2,1,0:T(8,128)(2,1)S(1)}, bf16[1,196,768]{2,1,0:T(8,128)(2,1)}, u32[]{:S(2)}) copy-start(bf16[1,196,768]{2,1,0:T(8,128)(2,1)} %param.9) | copy-start | bytes 903172
  7.2 82.9 %all-gather.2.cloned.1.call-start = ((), (), s32[]{:S(2)}) async-start(), calls=%async_computation.8 | async-start | bytes 2949120 | tf_op jit(solution)/shard_map/all_gather | solution.py:112
  95.1 11.8 %all-to-all-start.2 = ((bf16[4,2,64,768]{3,2,1,0:T(8,128)(2,1)}), bf16[4,2,64,768]{3,2,1,0:T(8,128)(2,1)S(1)}, u32[]{:S(2)}, u32[]{:S(2)}) async-start(bf16[4,2,64,768]{3,2,1,0:T(8,128)(2,1)} %pad_maximum_fusion), calls=%async_computation.2 | async-start | bytes 1572864 | tf_op jit(solution)/shard_map/all_to_all | solution.py:21
  98.6 68.9 %reduce-scatter.2.cloned.1.call-start = ((), (), s32[]{:S(2)}) async-start(), calls=%async_computation.9 | async-start | bytes 2949120 | tf_op jit(solution)/shard_map/reduce_scatter | solution.py:141
  167.4 4.4 %copy-start.1 = (bf16[1,384,768]{2,1,0:T(8,128)(2,1)S(1)}, bf16[1,384,768]{2,1,0:T(8,128)(2,1)}, u32[]{:S(2)}) copy-start(bf16[1,384,768]{2,1,0:T(8,128)(2,1)} %reduce-scatter.2.cloned.1.call-done) | copy-start | bytes 1769476
  168.1 24.5 %all-to-all-start.5 = ((bf16[16,2,384]{2,1,0:T(2,128)(2,1)}), bf16[16,2,384]{2,1,0:T(2,128)(2,1)S(1)}, u32[]{:S(2)}, u32[]{:S(2)}) async-start(bf16[16,2,384]{2,1,0:T(2,128)(2,1)} %broadcast_in_dim.13), calls=%async_computation.6 | async-start | bytes 49152 | tf_op jit(solution)/shard_map/all_to_all | solution.py:21
Sparse Core Ops, SparseCore 0:
  11.3 50.4 all-gather.1
  107.0 23.8 reduce-scatter.1
